TPU v7x, 32 devices: a whole 2x2x4 slice. The times are simulated.
32 devices in a mesh: rows: 16 (over z, y, x), cols: 2 (over core).
Axes of the slice: x: 2, y: 2, z: 4, core: 2. Of those that a mesh axis runs over, the one named last changes fastest.
Arguments:
- points: float32 [8192, 768], P('rows'), may hold values from -83 to 83
- landmark_index: int32 [4096], P('rows'), may hold values from 0 to 8191, as said below
- targets: float32 [4096, 512], P('rows', 'cols'), may hold values from -6 to 6
- ridge_shift: float32 [1], replicated, may hold values from 0.5 to 2
Outputs:
- projected: float32 [512, 2048], P('rows', 'cols')
- panels: float32 [4096, 256], P('rows')
- remainder: float32 [4096, 1792], P('rows', 'cols')
Inputs may be any that keep to these rules, and one draw needn't show every extreme that they name: `landmark_index`: landmark i is a point of the block [(i // 256) * 512, (i // 256 + 1) * 512); the 256 landmarks of one block are distinct.
All inputs are finite; a program needn't handle non-finite values.
Results may differ from a plain program's by a relative error of at most 0.00028.
Values sent between devices are 32-bit elements; how exact they have to be, the bound alone decides.
A program may use at most 64 MiB of HBM per device.

v0:
```python
import jax
import jax.numpy as jnp
from jax import lax
from jax.sharding import PartitionSpec as P

C = 2048
PW = 128


exact_mode = lax.Precision.HIGHEST


def spread(block, axis, source):
    block = jnp.where(lax.axis_index(axis) == source, block, jnp.zeros_like(block))
    return lax.psum(block, axis)


def gaussian(left_rows, right_rows):
    left_sq = jnp.sum(left_rows * left_rows, axis=1)
    right_sq = jnp.sum(right_rows * right_rows, axis=1)
    cross_term = jnp.dot(
        left_rows, right_rows.T, precision=exact_mode, preferred_element_type=jnp.float32
    )
    return jnp.exp(
        -(left_sq[:, None] + right_sq[None, :] - 2.0 * cross_term) / (2.0 * left_rows.shape[1])
    )


def product(left_rows, right_rows):
    return jnp.dot(
        left_rows, right_rows.T, precision=exact_mode, preferred_element_type=jnp.float32
    )


def per_device(points, landmark_index, targets, ridge_shift):
    rows_here = landmark_index.shape[0]
    block_points = points.shape[0]
    row_pos = lax.axis_index("rows")
    col_pos = lax.axis_index("cols")
    n_rows = lax.axis_size("rows")
    half_cols = C // 2
    quarter = half_cols // n_rows
    local_index = landmark_index - row_pos * block_points
    embedded = jnp.take(points, local_index, axis=0)
    own_landmarks = lax.dynamic_slice_in_dim(embedded, col_pos * quarter, quarter, 0)
    column_emb = lax.all_gather(own_landmarks, "rows", axis=0, tiled=True)
    row_ids = lax.broadcasted_iota(jnp.int32, (rows_here, half_cols), 0)
    col_ids = lax.broadcasted_iota(jnp.int32, (rows_here, half_cols), 1)
    offset = row_ids - col_pos * quarter
    ridge_hits = (offset >= 0) & (offset < quarter) & (col_ids == row_pos * quarter + offset)
    kernel_slab = gaussian(embedded, column_emb) + jnp.where(ridge_hits, ridge_shift[0], 0.0)
    all_targets = lax.all_gather(targets, "cols", axis=1, tiled=True)
    projected = lax.psum_scatter(
        lax.dot_general(
            all_targets,
            kernel_slab,
            (((0,), (0,)), ((), ())),
            precision=exact_mode,
            preferred_element_type=jnp.float32,
        ),
        "rows",
        scatter_dimension=0,
        tiled=True,
    )
    head_emb = column_emb[:PW]
    diag_base = gaussian(head_emb, head_emb) + ridge_shift[0] * jnp.eye(PW, dtype=jnp.float32)
    panel_list = []
    earlier = None
    for panel_index in range(2):
        diag_block = diag_base
        if panel_index == 1:
            diag_block = diag_block - product(earlier[:PW], earlier[:PW])
        diag_block = jnp.where(col_pos == panel_index, diag_block, jnp.eye(PW, dtype=jnp.float32))
        factor = jnp.linalg.cholesky(diag_block)
        local_panel = jax.scipy.linalg.solve_triangular(factor, kernel_slab[:, :PW].T, lower=True).T
        local_panel = spread(local_panel, "cols", panel_index)
        landmark_rows = lax.all_gather(
            lax.dynamic_slice_in_dim(local_panel, col_pos * quarter, quarter, 0),
            "rows",
            axis=0,
            tiled=True,
        )
        head_cols = kernel_slab[:, :PW] - product(local_panel, landmark_rows[:PW])
        tail_cols = kernel_slab[:, PW:] - product(local_panel, landmark_rows[PW:])
        kernel_slab = jnp.concatenate([head_cols, tail_cols], axis=1)
        panel_list.append(local_panel)
        earlier = landmark_rows
    return (projected, jnp.concatenate(panel_list, axis=1), kernel_slab[:, PW:])


def solution(mesh):
    in_specs = (P("rows", None), P("rows"), P("rows", "cols"), P())
    out_specs = (P("rows", "cols"), P("rows", None), P("rows", "cols"))
    return jax.shard_map(
        per_device, mesh=mesh, in_specs=in_specs, out_specs=out_specs, check_vma=False
    )
```

profile of v0, /device:TPU:0, one launch (start us, length us, event | category | flops | bytes accessed | tf_op | source)
XLA Modules:
  0.0 309.8 jit_solution(893794244863315785)
XLA Ops:
  8.6 1.1 gather_fusion
  11.4 70.9 %all-gather.2.cloned.1.call-done = f32[1024,768]{1,0:T(8,128)} async-done(((f32[64,768]{1,0:T(8,128)}), f32[1024,768]{1,0:T(8,128)}) %all-gather.2.cloned.1.call-update) | async-done | bytes 3145744 | tf_op jit(solution)/shard_map/all_gather | solution.py:46
  82.3 1.1 multiply_reduce_fusion.2
  83.4 1.6 convert_select_fusion
  85.1 11.7 %cholesky.44 = f32[128,128]{1,0:T(8,128)S(1)} custom-call(f32[128,128]{1,0:T(8,128)S(1)} %fusion.25), custom_call_target="Cholesky" | custom-call | tf_op jit(solution)/shard_map/jit(cholesky)/cholesky | solution.py:74
  98.2 9.8 %custom-call.6 = f32[1,128,128]{1,2,0:T(8,128)S(1)} custom-call(f32[1,128,128]{2,1,0:T(8,128)S(1)} %fusion.20), custom_call_target="InvertDiagBlocksLowerTriangular" | custom-call | tf_op jit(solution)/shard_map/jit(_solve_triangular)/triangular_solve | solution.py:75
  108.0 2.3 multiply_reduce_fusion
  110.9 3.0 fusion.4
  113.9 1.0 fusion.7
  114.9 3.8 %all_gather.13 = f32[256,512]{1,0:T(8,128)} all-gather(f32[256,256]{1,0:T(8,128)} %param.9), channel_id=1, replica_groups=mesh['rows'=16,'cols'=2] {'cols'}, dimensions={1}, use_global_device_ids=true | all-gather | bytes 786432 | tf_op jit(solution)/shard_map/all_gather | solution.py:52
  118.7 12.7 %all-reduce.3.cloned.1.call-done = f32[256,128]{0,1:T(8,128)} async-done(((f32[256,128]{0,1:T(8,128)}), f32[256,128]{0,1:T(8,128)}) %all-reduce.3.cloned.1.call-update) | async-done | bytes 131088 | tf_op jit(solution)/shard_map/psum | solution.py:15
  132.4 44.2 %all_gather.14 = f32[1024,128]{1,0:T(8,128)S(1)} all-gather(f32[64,128]{1,0:T(8,128)S(1)} %copy.15), channel_id=1, replica_groups=mesh['rows'=16,'cols'=2] {'rows'}, dimensions={0}, use_global_device_ids=true | all-gather | bytes 557056 | tf_op jit(solution)/shard_map/all_gather | solution.py:77
  177.0 11.7 %cholesky.55 = f32[128,128]{1,0:T(8,128)S(1)} custom-call(f32[128,128]{1,0:T(8,128)S(1)} %fusion.23), custom_call_target="Cholesky" | custom-call | tf_op jit(solution)/shard_map/jit(cholesky)/cholesky | solution.py:74
  190.1 9.8 %custom-call.7 = f32[1,128,128]{1,2,0:T(8,128)S(1)} custom-call(f32[1,128,128]{2,1,0:T(8,128)S(1)} %fusion.21), custom_call_target="InvertDiagBlocksLowerTriangular" | custom-call | tf_op jit(solution)/shard_map/jit(_solve_triangular)/triangular_solve | solution.py:75
  199.9 1.3 fusion.5
  201.2 1.0 fusion.6
  202.2 4.2 %convolution_bitcast_fusion = f32[512,1024]{0,1:T(8,128)} fusion(f32[256,1024]{1,0:T(8,128)S(1)} %fusion.4, f32[256,512]{1,0:T(8,128)} %all_gather.13), kind=kOutput, calls=%fused_computation.2 | convolution fusion | flops 1610612736 | bytes 3670016 | tf_op jit(solution)/shard_map/dot_general | solution.py:54
  206.4 2.9 copy.23
  209.4 2.1 convolution_subtract_fusion.1
  211.5 4.6 %all-reduce.5.cloned.1.call-done = f32[256,128]{0,1:T(8,128)} async-done(((f32[256,128]{0,1:T(8,128)}), f32[256,128]{0,1:T(8,128)}) %all-reduce.5.cloned.1.call-update) | async-done | bytes 131088 | tf_op jit(solution)/shard_map/psum | solution.py:15
  217.1 1.0 pad_maximum_fusion
  218.9 47.2 %all_gather.15 = f32[1024,128]{1,0:T(8,128)S(1)} all-gather(f32[64,128]{1,0:T(8,128)S(1)} %copy.18), channel_id=1, replica_groups=mesh['rows'=16,'cols'=2] {'rows'}, dimensions={0}, use_global_device_ids=true | all-gather | bytes 557056 | tf_op jit(solution)/shard_map/all_gather | solution.py:77
  266.2 2.9 convolution_subtract_fusion
  269.0 34.2 %reduce-scatter.4.cloned.1.call-done = f32[32,1024]{1,0:T(8,128)} async-done(((f32[512,1024]{1,0:T(8,128)}), f32[32,1024]{1,0:T(8,128)}) %reduce-scatter.4.cloned.1.call-update) | async-done | bytes 131088
  (36 shorter events, 9.0 us)
Async XLA Ops:
  7.2 1.4 copy-start
  7.2 75.1 %all-gather.2.cloned.1.call-start = ((), (), s32[]{:S(2)}) async-start(), calls=%async_computation.1 | async-start | bytes 3342336 | tf_op jit(solution)/shard_map/all_gather | solution.py:46
  10.6 120.8 %all-reduce.3.cloned.1.call-start = ((), (), s32[]{:S(2)}) async-start(), calls=%async_computation.2 | async-start | bytes 262144 | tf_op jit(solution)/shard_map/psum | solution.py:15
  108.0 2.8 copy-start.1
  114.9 101.2 %all-reduce.5.cloned.1.call-start = ((), (), s32[]{:S(2)}) async-start(), calls=%async_computation.3 | async-start | bytes 262144 | tf_op jit(solution)/shard_map/psum | solution.py:15
  176.6 32.7 %copy-start.2 = (f32[1024,128]{1,0:T(8,128)}, f32[1024,128]{1,0:T(8,128)S(1)}, u32[]{:S(2)}) copy-start(f32[1024,128]{1,0:T(8,128)S(1)} %all_gather.14) | copy-start | bytes 1572868
  202.2 101.1 %reduce-scatter.4.cloned.1.call-start = ((), (), s32[]{:S(2)}) async-start(), calls=%async_computation.4 | async-start | bytes 2228224
Sparse Core Ops, SparseCore 0:
  11.4 70.8 all-gather.1
  115.0 16.3 all-reduce.2
  202.3 13.7 all-reduce.4
  218.8 84.4 reduce-scatter.3
where the time goes:
time: 310 us
  waiting for transfers between devices  123 us (40%)
  blocking collectives  95.2 us (31%)
  other arithmetic  51.2 us (17%)
  matrix products  17.3 us (6%)
  between operations  14.6 us (5%)
  local copies, waits for them, and re-layouts  8.79 us (3%)
    all_gather x2, blocking collectives, per_device(): lax.all_gather(lax.dynamic_slice_in_dim(local_panel, col_pos * quarter, q...  91.4 us
    all_gather x1, waiting for transfers between devices, per_device(): column_emb = lax.all_gather(own_landmarks, 'rows', axis=0, tiled=True)  70.9 us
    unnamed x5, waiting for transfers between devices  34.3 us
    another operation x6, other arithmetic, per_device(): factor = jnp.linalg.cholesky(diag_block)  24.8 us
    another operation x4, other arithmetic, per_device(): jax.scipy.linalg.solve_triangular(factor, kernel_slab[:, :PW].T, lower=True)  20.9 us
    psum x2, waiting for transfers between devices, spread(): return lax.psum(block, axis)  17.3 us
    dot_general x4, matrix products, product(): jnp.dot(left_rows, right_rows.T, precision=exact_mode, preferred_element_...  6.57 us
  transfers between devices with their start and end apart: 4, of which 4 were waited for; matrix products, arithmetic and copies ran while one was open for 5% of the time, Pallas kernels for 0%

commit v1 on v0

v1 whole, which is shorter than its diff:
```python
import jax
import jax.numpy as jnp
from jax import lax
from jax.sharding import PartitionSpec as P

C = 2048
PW = 128

exact_mode = lax.Precision.HIGHEST


def dot_t(left, right):
    return lax.dot_general(
        left, right, (((1,), (1,)), ((), ())), precision=exact_mode, preferred_element_type=jnp.float32
    )


def gaussian(left_rows, right_rows):
    left_sq = jnp.sum(left_rows * left_rows, axis=1)
    right_sq = jnp.sum(right_rows * right_rows, axis=1)
    cross_term = dot_t(left_rows, right_rows)
    return jnp.exp(
        -(left_sq[:, None] + right_sq[None, :] - 2.0 * cross_term) / (2.0 * left_rows.shape[1])
    )


def inverse_factor(block):
    factor = jnp.linalg.cholesky(block)
    eye = jnp.eye(block.shape[0], dtype=jnp.float32)
    return jax.scipy.linalg.solve_triangular(factor, eye, lower=True)


def per_device(points, landmark_index, targets, ridge_shift):
    rows_here = landmark_index.shape[0]
    block_points = points.shape[0]
    row_pos = lax.axis_index("rows")
    col_pos = lax.axis_index("cols")
    n_rows = lax.axis_size("rows")
    half_cols = C // 2
    quarter = half_cols // n_rows
    ridge = ridge_shift[0]
    local_index = landmark_index - row_pos * block_points
    embedded = jnp.take(points, local_index, axis=0)
    own_landmarks = lax.dynamic_slice_in_dim(embedded, col_pos * quarter, quarter, 0)
    column_emb = lax.all_gather(own_landmarks, "rows", axis=0, tiled=True)
    heads = lax.all_gather(column_emb[:PW], "cols", axis=0, tiled=True)
    all_targets = lax.all_gather(targets, "cols", axis=1, tiled=True)

    row_ids = lax.broadcasted_iota(jnp.int32, (rows_here, half_cols), 0)
    col_ids = lax.broadcasted_iota(jnp.int32, (rows_here, half_cols), 1)
    offset = row_ids - col_pos * quarter
    ridge_hits = (offset >= 0) & (offset < quarter) & (col_ids == row_pos * quarter + offset)
    kernel_slab = gaussian(embedded, column_emb) + jnp.where(ridge_hits, ridge, 0.0)
    projected = lax.psum_scatter(
        lax.dot_general(
            all_targets,
            kernel_slab,
            (((0,), (0,)), ((), ())),
            precision=exact_mode,
            preferred_element_type=jnp.float32,
        ),
        "rows",
        scatter_dimension=0,
        tiled=True,
    )

    base = gaussian(heads, heads) + ridge * jnp.eye(2 * PW, dtype=jnp.float32)
    inv0 = inverse_factor(base[:PW, :PW])
    low = dot_t(base[PW:, :PW], inv0)
    inv1 = inverse_factor(base[PW:, PW:] - dot_t(low, low))

    hrow = lax.broadcasted_iota(jnp.int32, (rows_here, 2 * PW), 0)
    hcol = lax.broadcasted_iota(jnp.int32, (rows_here, 2 * PW), 1)
    hblock = hcol // PW
    hoff = hrow - hblock * quarter
    head_hits = (hoff >= 0) & (hoff < quarter) & (hcol - hblock * PW == row_pos * quarter + hoff)
    head_slab = gaussian(embedded, heads) + jnp.where(head_hits, ridge, 0.0)

    lrow = lax.broadcasted_iota(jnp.int32, (half_cols, 2 * PW), 0)
    lcol = lax.broadcasted_iota(jnp.int32, (half_cols, 2 * PW), 1)
    land_slab = gaussian(column_emb, heads) + jnp.where(
        (lrow < PW) & (lcol == col_pos * PW + lrow), ridge, 0.0
    )

    def panels_of(slab):
        first = dot_t(slab[:, :PW], inv0)
        second = dot_t(slab[:, PW:] - dot_t(first, low), inv1)
        return jnp.concatenate([first, second], axis=1)

    panels = panels_of(head_slab)
    land_panels = panels_of(land_slab)
    remainder = kernel_slab[:, PW:] - dot_t(panels, land_panels[PW:])
    return (projected, panels, remainder)


def solution(mesh):
    in_specs = (P("rows", None), P("rows"), P("rows", "cols"), P())
    out_specs = (P("rows", "cols"), P("rows", None), P("rows", "cols"))
    return jax.shard_map(
        per_device, mesh=mesh, in_specs=in_specs, out_specs=out_specs, check_vma=False
    )
```

time: 310 us -> 199 us (0.64)
  blocking collectives: 95.2 us -> 4.75 us
  waiting for transfers between devices: 123 us -> 89.6 us
  matrix products: 17.3 us -> 24.8 us
    all_gather x2 -> x1, blocking collectives: 91.4 us -> 2.37 us  [per_device(): heads = lax.all_gather(column_emb[:PW], 'cols', axis=0, tiled=True)]
    psum x2 -> x0, waiting for transfers between devices: 17.3 us -> none  [spread(): return lax.psum(block, axis)]
    unnamed x5 -> x3, waiting for transfers between devices: 34.3 us -> 23.4 us
    dot_general x6 -> x13, matrix products: 11.2 us -> 21 us  [dot_t(): lax.dot_general(left, right, (((1,), (1,)), ((), ())), precision=exact_mo...]
    all_gather x1, waiting for transfers between devices: 70.9 us -> 66.2 us  [per_device(): column_emb = lax.all_gather(own_landmarks, 'rows', axis=0, tiled=True)]
    unnamed x8 -> x30, local copies, waits for them, and re-layouts: 4.86 us -> 8.05 us
  transfers between devices with their start and end apart: 4 -> 2, of which waited for: 4 -> 2; matrix products, arithmetic and copies ran while one was open for 5% -> 28% of each run, Pallas kernels for 0% -> 0%
where the time goes in v1:
time: 199 us
  waiting for transfers between devices  89.6 us (45%)
  other arithmetic  53.3 us (27%)
  matrix products  24.8 us (12%)
  between operations  15 us (8%)
  local copies, waits for them, and re-layouts  11 us (6%)
  blocking collectives  4.75 us (2%)
    all_gather x1, waiting for transfers between devices, per_device(): column_emb = lax.all_gather(own_landmarks, 'rows', axis=0, tiled=True)  66.2 us
    another operation x6, other arithmetic, inverse_factor(): factor = jnp.linalg.cholesky(block)  25.6 us
    unnamed x3, waiting for transfers between devices  23.4 us
    dot_general x13, matrix products, dot_t(): lax.dot_general(left, right, (((1,), (1,)), ((), ())), precision=exact_mo...  21 us
    another operation x4, other arithmetic, inverse_factor(): return jax.scipy.linalg.solve_triangular(factor, eye, lower=True)  20.9 us
    unnamed x30, local copies, waits for them, and re-layouts  8.05 us
  transfers between devices with their start and end apart: 2, of which 2 were waited for; matrix products, arithmetic and copies ran while one was open for 28% of the time, Pallas kernels for 0%

profile of v1, /device:TPU:0, one launch (start us, length us, event | category | flops | bytes accessed | tf_op | source)
XLA Modules:
  0.0 198.5 jit_solution(4081377383036274796)
XLA Ops:
  8.6 1.1 gather_fusion
  9.9 0.9 copy-done.2
  14.0 2.4 %all_gather.10 = f32[256,512]{1,0:T(8,128)} all-gather(f32[256,256]{1,0:T(8,128)S(1)} %copy-done.13), channel_id=1, replica_groups=mesh['rows'=16,'cols'=2] {'cols'}, dimensions={1}, use_global_device_ids=true | all-gather | bytes 786432 | tf_op jit(solution)/shard_map/all_gather | solution.py:47
  16.4 66.2 %all-gather.2.cloned.1.call-done = f32[1024,768]{1,0:T(8,128)} async-done(((f32[64,768]{1,0:T(8,128)}), f32[1024,768]{1,0:T(8,128)}) %all-gather.2.cloned.1.call-update) | async-done | bytes 3145744 | tf_op jit(solution)/shard_map/all_gather | solution.py:45
  82.6 1.0 slice.50
  83.6 2.4 %all_gather.11 = f32[256,768]{1,0:T(8,128)S(1)} all-gather(f32[128,768]{1,0:T(8,128)S(1)} %slice.50), channel_id=1, replica_groups=mesh['rows'=16,'cols'=2] {'cols'}, dimensions={0}, use_global_device_ids=true | all-gather | bytes 1179648 | tf_op jit(solution)/shard_map/all_gather | solution.py:46
  87.1 11.7 %cholesky.44 = f32[128,128]{1,0:T(8,128)S(1)} custom-call(f32[128,128]{1,0:T(8,128)S(1)} %fusion.45), custom_call_target="Cholesky" | custom-call | tf_op jit(solution)/shard_map/jit(cholesky)/cholesky | solution.py:28
  99.5 2.4 %multiply_reduce_fusion = f32[1024]{0:T(1024)S(1)} fusion(f32[1024,768]{1,0:T(8,128)} %all-gather.2.cloned.1.call-done), kind=kLoop, calls=%fused_computation.1 | loop fusion | flops 1571840 | bytes 3149824 | tf_op jit(solution)/shard_map/reduce_sum | solution.py:20
  102.0 4.2 %fusion.9 = f32[256,1024]{1,0:T(8,128)S(1)} fusion(f32[256,768]{1,0:T(8,128)} %copy-done.2, f32[1024,768]{1,0:T(8,128)S(1)} %copy-done.1, f32[]{:T(128)} %bitcast.45, s32[256]{0:T(256)S(1)} %fusion.46, f32[1024]{0:T(1024)S(1)} %multiply_reduce_fusion, f32[256]{0:T(256)S(1)} %get-tuple-element.11, pred[256]{0:T(512)(128)(4,1)S(1)} %compare_and_fusion.1), kind=kOutput, calls=%fused_computation.14 | convolution fusion | flops 2418278400 | bytes 4987140 | tf_op jit(solution)/shard_map/dot_general | solution.py:13
  106.2 3.2 %convolution_bitcast_fusion = f32[512,1024]{0,1:T(8,128)} fusion(f32[256,1024]{1,0:T(8,128)S(1)} %fusion.9, f32[256,512]{1,0:T(8,128)S(1)} %copy-done.3), kind=kOutput, calls=%fused_computation.2 | convolution fusion | flops 1610612736 | bytes 3670016 | tf_op jit(solution)/shard_map/dot_general | solution.py:55
  109.4 2.9 %copy.24 = f32[512,1024]{1,0:T(8,128)} copy(f32[512,1024]{0,1:T(8,128)} %convolution_bitcast_fusion) | data formatting | bytes 4194304
  113.0 9.8 %custom-call.6 = f32[1,128,128]{1,2,0:T(8,128)S(1)} custom-call(f32[1,128,128]{2,1,0:T(8,128)S(1)} %fusion.38), custom_call_target="InvertDiagBlocksLowerTriangular" | custom-call | tf_op jit(solution)/shard_map/jit(_solve_triangular)/triangular_solve | solution.py:30
  123.7 1.1 fusion.40
  125.5 1.1 convolution_subtract_fusion.3
  127.3 12.5 %cholesky.55 = f32[128,128]{1,0:T(8,128)S(1)} custom-call(f32[128,128]{1,0:T(8,128)} %fusion.43), custom_call_target="Cholesky" | custom-call | tf_op jit(solution)/shard_map/jit(cholesky)/cholesky | solution.py:28
  141.2 9.8 %custom-call.7 = f32[1,128,128]{1,2,0:T(8,128)S(1)} custom-call(f32[1,128,128]{2,1,0:T(8,128)S(1)} %fusion.39), custom_call_target="InvertDiagBlocksLowerTriangular" | custom-call | tf_op jit(solution)/shard_map/jit(_solve_triangular)/triangular_solve | solution.py:30
  151.3 2.0 %fusion.15 = f32[256,256]{0,1:T(8,128)S(1)} fusion(f32[256,768]{1,0:T(8,128)} %copy-done.2, f32[256,768]{1,0:T(8,128)S(1)} %all_gather.11, f32[]{:T(128)} %bitcast.46, s32[]{:T(128)S(6)} %mul.65, s32[256]{0:T(256)} %get-tuple-element.15, s32[256]{0:T(256)} %get-tuple-element.16, f32[256]{0:T(256)S(1)} %multiply_reduce_fusion.1, ...), kind=kOutput, calls=%fused_computation.24 | convolution fusion | flops 605159424 | bytes 1839368 | tf_op jit(solution)/shard_map/dot_general | solution.py:13
  153.4 1.1 fusion.32
  154.5 1.1 convolution_subtract_fusion.2
  157.3 1.8 copy.20
  159.1 5.0 %fusion.4 = f32[1024,256]{1,0:T(8,128)S(1)} fusion(f32[1024,768]{1,0:T(8,128)} %all-gather.2.cloned.1.call-done, f32[256,768]{1,0:T(8,128)S(1)} %all_gather.11, f32[]{:T(128)} %bitcast.47, s32[1024]{0:T(1024)S(1)} %iota_add_fusion, f32[256]{0:T(256)S(1)} %multiply_reduce_fusion.1, f32[1024]{0:T(1024)S(1)} %multiply_reduce_fusion, ...), kind=kOutput, calls=%fused_computation.8 | convolution fusion | flops 2418278400 | bytes 4990980 | tf_op jit(solution)/shard_map/dot_general | solution.py:13
  164.7 1.0 convolution_subtract_fusion.1
  166.3 2.0 convolution_subtract_fusion
  168.3 23.4 %reduce-scatter.4.cloned.1.call-done = f32[32,1024]{1,0:T(8,128)} async-done(((f32[512,1024]{1,0:T(8,128)}), f32[32,1024]{1,0:T(8,128)}) %reduce-scatter.4.cloned.1.call-update) | async-done | bytes 131088
  (60 shorter events, 13.3 us)
Async XLA Ops:
  7.2 1.4 copy-start
  7.2 75.4 %all-gather.2.cloned.1.call-start = ((), (), s32[]{:S(2)}) async-start(), calls=%async_computation.1 | async-start | bytes 3342336 | tf_op jit(solution)/shard_map/all_gather | solution.py:45
  8.6 5.4 %copy-start.13 = (f32[256,256]{1,0:T(8,128)S(1)}, f32[256,256]{1,0:T(8,128)}, u32[]{:S(2)}) copy-start(f32[256,256]{1,0:T(8,128)} %param.9) | copy-start | bytes 786436
  9.9 0.9 copy-start.2
  11.5 180.2 %reduce-scatter.4.cloned.1.call-start = ((), (), s32[]{:S(2)}) async-start(), calls=%async_computation.2 | async-start | bytes 2228224
  87.0 15.0 %copy-start.8 = (f32[256,256]{0,1:T(8,128)}, f32[256,256]{0,1:T(8,128)S(1)}, u32[]{:S(2)}) copy-start(f32[256,256]{0,1:T(8,128)S(1)} %fusion.19) | copy-start | bytes 786436
  98.8 3.1 %copy-start.1 = (f32[1024,768]{1,0:T(8,128)S(1)}, f32[1024,768]{1,0:T(8,128)}, u32[]{:S(2)}) copy-start(f32[1024,768]{1,0:T(8,128)} %all-gather.2.cloned.1.call-done) | copy-start | bytes 9437188
  101.9 4.2 %copy-start.3 = (f32[256,512]{1,0:T(8,128)S(1)}, f32[256,512]{1,0:T(8,128)}, u32[]{:S(2)}) copy-start(f32[256,512]{1,0:T(8,128)} %all_gather.10) | copy-start | bytes 1572868
  123.1 0.6 copy-start.9
  124.9 0.6 copy-start.4
  151.3 4.3 %copy-start.11 = (f32[128,128]{1,0:T(8,128)}, f32[128,128]{1,0:T(8,128)S(1)}, u32[]{:S(2)}) copy-start(f32[128,128]{1,0:T(8,128)S(1)} %fusion.34) | copy-start | bytes 196612
  155.9 0.6 copy-start.6
  159.1 5.0 %copy-start.10 = (f32[128,128]{1,0:T(8,128)S(1)}, f32[128,128]{1,0:T(8,128)}, u32[]{:S(2)}) copy-start(f32[128,128]{1,0:T(8,128)} %copy-done.9) | copy-start | bytes 196612
  159.1 5.6 %copy-start.5 = (f32[128,128]{1,0:T(8,128)S(1)}, f32[128,128]{1,0:T(8,128)}, u32[]{:S(2)}) copy-start(f32[128,128]{1,0:T(8,128)} %copy-done.4) | copy-start | bytes 196612
  159.1 6.6 %copy-start.12 = (f32[128,128]{1,0:T(8,128)S(1)}, f32[128,128]{1,0:T(8,128)}, u32[]{:S(2)}) copy-start(f32[128,128]{1,0:T(8,128)} %copy-done.11) | copy-start | bytes 196612
  164.1 2.3 %copy-start.7 = (f32[256,128]{0,1:T(8,128)S(1)}, f32[256,128]{0,1:T(8,128)}, u32[]{:S(2)}) copy-start(f32[256,128]{0,1:T(8,128)} %copy-done.6) | copy-start | bytes 393220
Sparse Core Ops, SparseCore 0:
  11.6 70.8 all-gather.1
  112.5 79.1 reduce-scatter.3

commit v2 on v1

--- a/solution.py
+++ b/solution.py
@@ -1,6 +1,8 @@
 import jax
 import jax.numpy as jnp
 from jax import lax
+from jax.experimental import pallas as pl
+from jax.experimental.pallas import tpu as pltpu
 from jax.sharding import PartitionSpec as P
 
 C = 2048
@@ -28,6 +30,171 @@
     factor = jnp.linalg.cholesky(block)
     eye = jnp.eye(block.shape[0], dtype=jnp.float32)
     return jax.scipy.linalg.solve_triangular(factor, eye, lower=True)
+
+
+MESH = pl.DeviceIdType.MESH
+PLANE = 4
+
+
+def gather_kernel(emb_ref, tgt_ref, col_ref, head_ref, all_tgt_ref, send, recv):
+    r = lax.axis_index("rows")
+    c = lax.axis_index("cols")
+    n_rows = lax.axis_size("rows")
+    lines = n_rows // PLANE
+    line, q = r // PLANE, r % PLANE
+    quarter = col_ref.shape[0] // n_rows
+    half = col_ref.shape[1] // 2
+    x = line * PLANE + (q + 1 - 2 * (q % 2))
+    y = line * PLANE + (q + 2) % PLANE
+    qx, qy = q + 1 - 2 * (q % 2), (q + 2) % PLANE
+    up, down = r + PLANE, r - PLANE
+    has_up, has_down = line < lines - 1, line > 0
+    core = (r, 1 - c)
+
+    def rows_of(t, who):
+        return pl.ds(pl.multiple_of((t * PLANE + who) * quarter, quarter), quarter)
+
+    own = emb_ref.at[pl.ds(pl.multiple_of(c * quarter, quarter), quarter)]
+
+    def remote(src, dst, kind, t, dev):
+        return pltpu.make_async_remote_copy(
+            src_ref=src, dst_ref=dst, send_sem=send.at[kind, t], recv_sem=recv.at[kind, t],
+            device_id=dev, device_id_type=MESH,
+        )
+
+    def whole(kind, t, who, dev, first=False):
+        dst = col_ref.at[rows_of(t, who)]
+        return remote(own if first else dst, dst, kind, t, dev)
+
+    def part(kind, t, who, side, dev):
+        dst = col_ref.at[rows_of(t, who), pl.ds(side * half, half)]
+        return remote(dst, dst, kind, t, dev)
+
+    barrier = pltpu.get_barrier_semaphore()
+    for dev in ((x, c), (y, c), core):
+        pl.semaphore_signal(barrier, inc=1, device_id=dev, device_id_type=MESH)
+
+    @pl.when(has_up)
+    def _():
+        pl.semaphore_signal(barrier, inc=1, device_id=(up, c), device_id_type=MESH)
+
+    @pl.when(has_down)
+    def _():
+        pl.semaphore_signal(barrier, inc=1, device_id=(down, c), device_id_type=MESH)
+
+    pl.semaphore_wait(barrier, 3 + jnp.where(has_up, 1, 0) + jnp.where(has_down, 1, 0))
+
+    def send_on(t, first=False):
+        whole(2, t, q, (x, c), first).start()
+        whole(3, t, q, (y, c), first).start()
+
+    own_copy = pltpu.make_async_copy(own, col_ref.at[rows_of(line, q)], send.at[7, 0])
+    tgt_copy = pltpu.make_async_copy(tgt_ref, all_tgt_ref.at[c], send.at[7, 1])
+
+    @pl.when(has_up)
+    def _():
+        whole(0, line, q, (up, c), True).start()
+
+    @pl.when(has_down)
+    def _():
+        whole(1, line, q, (down, c), True).start()
+
+    send_on(line, True)
+    own_copy.start()
+    tgt_copy.start()
+    tgt_swap = remote(tgt_ref, all_tgt_ref.at[c], 6, 0, core)
+    tgt_swap.start()
+
+    def ring_stage(t):
+        whole(2, t, qx, (x, c)).wait_recv()
+        part(5, t, qx, 0, (y, c)).start()
+        whole(3, t, qy, (y, c)).wait_recv()
+        part(4, t, qy, 1, (x, c)).start()
+
+    for step in range(1, lines + 1):
+        if step < lines:
+            @pl.when(line - step >= 0)
+            def _(step=step):
+                t = line - step
+                whole(0, t, q, (up, c)).wait_recv()
+
+                @pl.when(has_up)
+                def _():
+                    whole(0, t, q, (up, c)).start()
+
+                send_on(t)
+
+            @pl.when(line + step < lines)
+            def _(step=step):
+                t = line + step
+                whole(1, t, q, (down, c)).wait_recv()
+
+                @pl.when(has_down)
+                def _():
+                    whole(1, t, q, (down, c)).start()
+
+                send_on(t)
+
+        if step == 1:
+            ring_stage(line)
+        else:
+            @pl.when(line - (step - 1) >= 0)
+            def _(step=step):
+                ring_stage(line - (step - 1))
+
+            @pl.when(line + (step - 1) < lines)
+            def _(step=step):
+                ring_stage(line + (step - 1))
+
+    opposite = (q + 2 - 4 * (q // 2)) + 1 - 2 * (q % 2)
+    for t in range(lines):
+        part(4, t, opposite, 1, (x, c)).wait_recv()
+        part(5, t, opposite, 0, (y, c)).wait_recv()
+    own_copy.wait()
+
+    heads = col_ref.at[pl.ds(0, PW)]
+    head_copy = pltpu.make_async_copy(heads, head_ref.at[c], send.at[7, 2])
+    head_swap = remote(heads, head_ref.at[c], 6, 1, core)
+    head_copy.start()
+    head_swap.start()
+
+    for t in range(lines):
+        whole(2, t, q, (x, c)).wait_send()
+        whole(3, t, q, (y, c)).wait_send()
+        part(4, t, qy, 1, (x, c)).wait_send()
+        part(5, t, qx, 0, (y, c)).wait_send()
+
+        @pl.when(has_up & (t <= line))
+        def _(t=t):
+            whole(0, t, q, (up, c)).wait_send()
+
+        @pl.when(has_down & (t >= line))
+        def _(t=t):
+            whole(1, t, q, (down, c)).wait_send()
+
+    tgt_copy.wait()
+    head_copy.wait()
+    remote(tgt_ref, all_tgt_ref.at[1 - c], 6, 0, core).wait()
+    remote(heads, head_ref.at[1 - c], 6, 1, core).wait()
+
+
+def gather(embedded, targets, n_rows):
+    width = embedded.shape[1]
+    return pl.pallas_call(
+        gather_kernel,
+        out_shape=(
+            jax.ShapeDtypeStruct((C // 2, width), jnp.float32),
+            jax.ShapeDtypeStruct((2, PW, width), jnp.float32),
+            jax.ShapeDtypeStruct((2,) + targets.shape, jnp.float32),
+        ),
+        in_specs=[pl.BlockSpec(memory_space=pl.ANY)] * 2,
+        out_specs=(pl.BlockSpec(memory_space=pl.ANY),) * 3,
+        scratch_shapes=[
+            pltpu.SemaphoreType.DMA((8, max(n_rows // PLANE, 3))),
+            pltpu.SemaphoreType.DMA((8, max(n_rows // PLANE, 3))),
+        ],
+        compiler_params=pltpu.CompilerParams(collective_id=0, has_side_effects=True),
+    )(embedded, targets)
 
 
 def per_device(points, landmark_index, targets, ridge_shift):
@@ -41,10 +208,9 @@
     ridge = ridge_shift[0]
     local_index = landmark_index - row_pos * block_points
     embedded = jnp.take(points, local_index, axis=0)
-    own_landmarks = lax.dynamic_slice_in_dim(embedded, col_pos * quarter, quarter, 0)
-    column_emb = lax.all_gather(own_landmarks, "rows", axis=0, tiled=True)
-    heads = lax.all_gather(column_emb[:PW], "cols", axis=0, tiled=True)
-    all_targets = lax.all_gather(targets, "cols", axis=1, tiled=True)
+    column_emb, head_pair, target_pair = gather(embedded, targets, n_rows)
+    heads = head_pair.reshape(2 * PW, -1)
+    all_targets = jnp.concatenate([target_pair[0], target_pair[1]], axis=1)
 
     row_ids = lax.broadcasted_iota(jnp.int32, (rows_here, half_cols), 0)
     col_ids = lax.broadcasted_iota(jnp.int32, (rows_here, half_cols), 1)

time: 199 us -> 157 us (0.79)
  waiting for transfers between devices: 89.6 us -> 18.2 us
  Pallas kernels: 0 us -> 47.5 us
  local copies, waits for them, and re-layouts: 11 us -> 5.2 us
  matrix products: 24.8 us -> 19.7 us
  blocking collectives: 4.75 us -> 0 us
  other arithmetic: 53.3 us -> 50.8 us
    all_gather x1 -> x0, waiting for transfers between devices: 66.2 us -> none  [per_device(): column_emb = lax.all_gather(own_landmarks, 'rows', axis=0, tiled=True)]
    pallas_call x0 -> x1, Pallas kernels: none -> 47.5 us  [gather(): pl.pallas_call(gather_kernel, out_shape=(jax.ShapeDtypeStruct((C // 2, wi...]
    unnamed x3 -> x1, waiting for transfers between devices: 23.4 us -> 0.02 us
    reduce_scatter x0 -> x1, waiting for transfers between devices: none -> 18.2 us  [per_device(): lax.psum_scatter(lax.dot_general(all_targets, kernel_slab, (((0,), (0,)),...]
    unnamed x30 -> x17, local copies, waits for them, and re-layouts: 8.05 us -> 1.87 us
    dot_general x13, matrix products: 21 us -> 15.9 us  [dot_t(): lax.dot_general(left, right, (((1,), (1,)), ((), ())), precision=exact_mo...]
    all_gather x2 -> x0, blocking collectives: 4.75 us -> none  [the longest x1 2.38 us: per_device(): all_targets = lax.all_gather(targets, 'cols', axis=1, tiled=True)]
  transfers between devices with their start and end apart: 2 -> 1, of which waited for: 2 -> 1; matrix products, arithmetic and copies ran while one was open for 28% -> 40% of each run, Pallas kernels for 0% -> 0%
where the time goes in v2:
time: 157 us
  other arithmetic  50.8 us (32%)
  Pallas kernels  47.5 us (30%)
  matrix products  19.7 us (13%)
  waiting for transfers between devices  18.2 us (12%)
  between operations  15.1 us (10%)
  local copies, waits for them, and re-layouts  5.2 us (3%)
    pallas_call x1, Pallas kernels, gather(): pl.pallas_call(gather_kernel, out_shape=(jax.ShapeDtypeStruct((C // 2, wi...  47.5 us
    another operation x6, other arithmetic, inverse_factor(): factor = jnp.linalg.cholesky(block)  24.8 us
    another operation x4, other arithmetic, inverse_factor(): return jax.scipy.linalg.solve_triangular(factor, eye, lower=True)  21.1 us
    reduce_scatter x1, waiting for transfers between devices, per_device(): lax.psum_scatter(lax.dot_general(all_targets, kernel_slab, (((0,), (0,)),...  18.2 us
    dot_general x13, matrix products, dot_t(): lax.dot_general(left, right, (((1,), (1,)), ((), ())), precision=exact_mo...  15.9 us
    dot_general x1, matrix products, per_device(): lax.dot_general(all_targets, kernel_slab, (((0,), (0,)), ((), ())), preci...  3.25 us
  transfers between devices with their start and end apart: 1, of which 1 were waited for; matrix products, arithmetic and copies ran while one was open for 40% of the time, Pallas kernels for 0%

profile of v2, /device:TPU:0, one launch (start us, length us, event | category | flops | bytes accessed | tf_op | source)
XLA Modules:
  0.0 156.6 jit_solution(14048212335860195221)
XLA Ops:
  8.0 0.7 compare_and_fusion.2
  8.7 1.1 gather_fusion
  9.8 1.0 multiply_reduce_fusion.2
  10.8 47.5 %shard_map.67 = (f32[1024,768]{1,0:T(8,128)}, f32[2,128,768]{2,1,0:T(8,128)}, f32[2,256,256]{2,1,0:T(8,128)}) custom-call(f32[256,768]{1,0:T(8,128)} %get-tuple-element.15.emb_ref, f32[256,256]{1,0:T(8,128)} %tgt_ref.1), custom_call_target="tpu_custom_call" | custom-call | tf_op jit(solution)/shard_map/pallas_call | solution.py:183
  58.3 1.2 slice_bitcast_fusion.1
  59.6 2.2 %multiply_reduce_fusion = f32[1024]{0:T(1024)S(1)} fusion(f32[1024,768]{1,0:T(8,128)} %get-tuple-element.9), kind=kLoop, calls=%fused_computation.1 | loop fusion | flops 1571840 | bytes 3149824 | tf_op jit(solution)/shard_map/reduce_sum | solution.py:22
  61.8 3.1 %fusion.9 = f32[256,1024]{1,0:T(8,128)S(1)} fusion(f32[256,768]{1,0:T(8,128)S(1)} %copy-done.3, f32[1024,768]{1,0:T(8,128)S(1)} %copy-done.1, f32[]{:T(128)} %bitcast.47, s32[256]{0:T(256)S(1)} %fusion.50, f32[1024]{0:T(1024)S(1)} %multiply_reduce_fusion, f32[256]{0:T(256)S(1)} %get-tuple-element.14, pred[256]{0:T(512)(128)(4,1)S(1)} %compare_and_fusion.1), kind=kOutput, calls=%fused_computation.13 | convolution fusion | flops 2418278400 | bytes 4987140 | tf_op jit(solution)/shard_map/dot_general | solution.py:15
  64.8 1.0 copy-done.4
  65.8 3.3 %fusion.25 = f32[512,1024]{1,0:T(8,128)} fusion(f32[256,1024]{1,0:T(8,128)S(1)} %fusion.9, f32[256,256]{1,0:T(8,128)S(1)} %get-tuple-element.19, f32[256,256]{1,0:T(8,128)S(1)} %get-tuple-element.18), kind=kOutput, calls=%fused_computation.40 | convolution fusion | flops 1610743808 | bytes 3670016 | tf_op jit(solution)/shard_map/dot_general | solution.py:221
  69.2 0.9 fusion.19
  70.2 11.7 %cholesky.44 = f32[128,128]{1,0:T(8,128)S(1)} custom-call(f32[128,128]{1,0:T(8,128)S(1)} %fusion.49), custom_call_target="Cholesky" | custom-call | tf_op jit(solution)/shard_map/jit(cholesky)/cholesky | solution.py:30
  82.6 0.7 fusion.42
  83.3 10.0 %custom-call.6 = f32[1,128,128]{1,2,0:T(8,128)S(1)} custom-call(f32[1,128,128]{2,1,0:T(8,128)S(1)} %fusion.42), custom_call_target="InvertDiagBlocksLowerTriangular" | custom-call | tf_op jit(solution)/shard_map/jit(_solve_triangular)/triangular_solve | solution.py:32
  93.8 0.9 convolution_subtract_fusion.3
  94.7 0.9 copy.11
  95.7 0.9 fusion.47
  96.5 11.7 %cholesky.55 = f32[128,128]{1,0:T(8,128)S(1)} custom-call(f32[128,128]{1,0:T(8,128)S(1)} %fusion.47), custom_call_target="Cholesky" | custom-call | tf_op jit(solution)/shard_map/jit(cholesky)/cholesky | solution.py:30
  109.6 9.8 %custom-call.7 = f32[1,128,128]{1,2,0:T(8,128)S(1)} custom-call(f32[1,128,128]{2,1,0:T(8,128)S(1)} %fusion.43), custom_call_target="InvertDiagBlocksLowerTriangular" | custom-call | tf_op jit(solution)/shard_map/jit(_solve_triangular)/triangular_solve | solution.py:32
  119.7 0.9 fusion.15
  121.5 0.8 copy.12
  122.3 4.9 %fusion.4 = f32[1024,256]{1,0:T(8,128)S(1)} fusion(f32[1024,768]{1,0:T(8,128)} %get-tuple-element.9, f32[256,768]{1,0:T(8,128)S(1)} %bitcast.53, f32[]{:T(128)} %bitcast.49, s32[1024]{0:T(1024)S(1)} %iota_add_fusion, f32[256]{0:T(256)S(1)} %bitcast.56, f32[1024]{0:T(1024)S(1)} %multiply_reduce_fusion, pred[1024]{0:T(1024)(128)(4,1)S(1)} %iota_compare_fusion.7), kind=kOutput, calls=%fused_computation.7 | convolution fusion | flops 2418278400 | bytes 4990980 | tf_op jit(solution)/shard_map/dot_general | solution.py:15
  127.9 1.0 convolution_subtract_fusion.1
  129.5 2.0 %convolution_subtract_fusion = f32[256,896]{1,0:T(8,128)} fusion(f32[1024,128]{0,1:T(8,128)S(1)} %fusion.54, f32[1024,128]{0,1:T(8,128)S(1)} %fusion.23, f32[256,1024]{1,0:T(8,128)S(1)} %copy-done.5, f32[256,128]{0,1:T(8,128)S(1)} %fusion.53, f32[256,128]{0,1:T(8,128)S(1)} %fusion.36), kind=kOutput, calls=%fused_computation.14 | convolution fusion | flops 705167360 | bytes 3145728 | tf_op jit(solution)/shard_map/dot_general | solution.py:15
  131.5 18.2 %reduce-scatter.2.cloned.1.call-done = f32[32,1024]{1,0:T(8,128)} async-done(((f32[512,1024]{1,0:T(8,128)}), f32[32,1024]{1,0:T(8,128)}) %reduce-scatter.2.cloned.1.call-update) | async-done | bytes 131088 | tf_op jit(solution)/shard_map/reduce_scatter | solution.py:220
  (42 shorter events, 5.3 us)
Async XLA Ops:
  7.2 1.6 copy-start
  7.2 142.5 %reduce-scatter.2.cloned.1.call-start = ((), (), s32[]{:S(2)}) async-start(), calls=%async_computation.1 | async-start | bytes 2228224 | tf_op jit(solution)/shard_map/reduce_scatter | solution.py:220
  10.8 50.9 %copy-start.3 = (f32[256,768]{1,0:T(8,128)S(1)}, f32[256,768]{1,0:T(8,128)}, u32[]{:S(2)}) copy-start(f32[256,768]{1,0:T(8,128)} %get-tuple-element.15.emb_ref) | copy-start | bytes 2359300
  58.3 3.4 %copy-start.1 = (f32[1024,768]{1,0:T(8,128)S(1)}, f32[1024,768]{1,0:T(8,128)}, u32[]{:S(2)}) copy-start(f32[1024,768]{1,0:T(8,128)} %get-tuple-element.9) | copy-start | bytes 9437188
  64.8 1.0 copy-start.4
  64.8 4.3 %copy-start.2 = (f32[2,128,768]{2,1,0:T(8,128)S(1)}, f32[2,128,768]{2,1,0:T(8,128)}, u32[]{:S(2)}) copy-start(f32[2,128,768]{2,1,0:T(8,128)} %get-tuple-element.10) | copy-start | bytes 2359300
  119.7 1.5 copy-start.6
  122.3 6.6 %copy-start.7 = (f32[128,128]{1,0:T(8,128)S(1)}, f32[128,128]{1,0:T(8,128)}, u32[]{:S(2)}) copy-start(f32[128,128]{1,0:T(8,128)} %copy-done.6) | copy-start | bytes 196612
  127.3 2.3 %copy-start.5 = (f32[256,1024]{1,0:T(8,128)S(1)}, f32[256,1024]{1,0:T(8,128)}, u32[]{:S(2)}) copy-start(f32[256,1024]{1,0:T(8,128)} %copy-done.4) | copy-start | bytes 3145732
Sparse Core Ops, SparseCore 0:
  69.2 80.4 reduce-scatter.1

commit v3 on v2

--- a/solution.py
+++ b/solution.py
@@ -7,6 +7,7 @@
 
 C = 2048
 PW = 128
+BLOCK = 32
 
 exact_mode = lax.Precision.HIGHEST
 
@@ -24,12 +25,6 @@
     return jnp.exp(
         -(left_sq[:, None] + right_sq[None, :] - 2.0 * cross_term) / (2.0 * left_rows.shape[1])
     )
-
-
-def inverse_factor(block):
-    factor = jnp.linalg.cholesky(block)
-    eye = jnp.eye(block.shape[0], dtype=jnp.float32)
-    return jax.scipy.linalg.solve_triangular(factor, eye, lower=True)
 
 
 MESH = pl.DeviceIdType.MESH
@@ -197,6 +192,254 @@
     )(embedded, targets)
 
 
+def head_gaussian(left_rows, heads, heads_sq):
+    left_sq = jnp.sum(left_rows * left_rows, axis=1, keepdims=True)
+    return jnp.exp(
+        -(left_sq + heads_sq - 2.0 * dot_t(left_rows, heads)) / (2.0 * left_rows.shape[1])
+    )
+
+
+def iota(shape, axis):
+    return lax.broadcasted_iota(jnp.int32, shape, axis)
+
+
+def eliminate(work, first, size):
+    n = work.shape[0]
+    start = pl.multiple_of(first * size, size)
+    rows = work[pl.ds(start, size), :]
+    rolled = pltpu.roll(rows, n - start, 1)
+    lane = iota((size, 128), 1)
+    row = iota((size, 128), 0)
+    pair = jnp.where(lane < size, rolled[:, :128], jnp.where(lane == row + size, 1.0, 0.0))
+    for j in range(size - 1):
+        column = pair[:, j : j + 1]
+        scaled = pair[j : j + 1, :] / pair[j : j + 1, j : j + 1]
+        pair = pair - jnp.where(row > j, column, 0.0) * scaled
+    diagonal = jnp.sum(jnp.where(lane == row, pair, 0.0), axis=1, keepdims=True)
+    block_inv = (pair / jnp.sqrt(diagonal))[:, size : 2 * size]
+
+    wide_lane = iota((size, n), 1) - start
+    inside = (wide_lane >= 0) & (wide_lane < size)
+    eye = jnp.where(wide_lane == iota((size, n), 0), 1.0, 0.0)
+    done = jnp.dot(
+        block_inv, jnp.where(inside, eye, rows), precision=exact_mode, preferred_element_type=jnp.float32
+    )
+    below = jnp.where(wide_lane >= size, done, 0.0)
+    update = lax.dot_general(
+        below, done, (((0,), (0,)), ((), ())), precision=exact_mode, preferred_element_type=jnp.float32
+    )
+    all_row = iota((n, n), 0) - start
+    all_lane = iota((n, n), 1) - start
+    keep = jnp.where((all_row >= size) & (all_lane >= 0) & (all_lane < size), 0.0, work[...])
+    work[...] = keep - update
+    work[pl.ds(start, size), :] = done
+
+
+def finish_kernel(
+    ridge_ref, part_ref, emb_ref, col_ref, head_ref, slab_ref, out_ref, panel_ref, rem_ref,
+    opp_x, opp_y, from_x, from_y, to_x, to_y, acc, from_down, from_up, work, land, head_slab, send, recv,
+):
+    r = lax.axis_index("rows")
+    c = lax.axis_index("cols")
+    n_rows = lax.axis_size("rows")
+    lines = n_rows // PLANE
+    line, q = r // PLANE, r % PLANE
+    qx, qy = q + 1 - 2 * (q % 2), (q + 2) % PLANE
+    opposite = PLANE - 1 - q
+    x, y = (line * PLANE + qx, c), (line * PLANE + qy, c)
+    up, down = (r + PLANE, c), (r - PLANE, c)
+    has_up, has_down = line < lines - 1, line > 0
+    wide = part_ref.shape[2]
+    half = wide // 2
+    lo, hi = pl.ds(0, half), pl.ds(half, half)
+    rows_here = emb_ref.shape[0]
+    half_cols = col_ref.shape[0]
+    quarter = half_cols // n_rows
+    n_head = head_ref.shape[0]
+    pw = n_head // 2
+    ridge = ridge_ref[0]
+
+    def remote(src, dst, kind, t, dev):
+        return pltpu.make_async_remote_copy(
+            src_ref=src, dst_ref=dst, send_sem=send.at[kind, t], recv_sem=recv.at[kind, t],
+            device_id=dev, device_id_type=MESH,
+        )
+
+    def c_opp_x(t):
+        return remote(part_ref.at[t * PLANE + opposite, :, lo], opp_x.at[t], 0, t, x)
+
+    def c_opp_y(t):
+        return remote(part_ref.at[t * PLANE + opposite, :, hi], opp_y.at[t], 1, t, y)
+
+    def c_plain_x(t):
+        return remote(part_ref.at[t * PLANE + qx, :, lo], from_x.at[t, :, lo], 2, t, x)
+
+    def c_plain_y(t):
+        return remote(part_ref.at[t * PLANE + qy, :, hi], from_y.at[t, :, hi], 3, t, y)
+
+    def c_sum_x(t):
+        return remote(to_x.at[t], from_x.at[t, :, hi], 4, t, x)
+
+    def c_sum_y(t):
+        return remote(to_y.at[t], from_y.at[t, :, lo], 5, t, y)
+
+    def c_up(t):
+        return remote(acc.at[t], from_down.at[t], 6, t, up)
+
+    def c_down(t):
+        return remote(acc.at[t], from_up.at[t], 7, t, down)
+
+    barrier = pltpu.get_barrier_semaphore()
+    for dev in (x, y):
+        pl.semaphore_signal(barrier, inc=1, device_id=dev, device_id_type=MESH)
+
+    @pl.when(has_up)
+    def _():
+        pl.semaphore_signal(barrier, inc=1, device_id=up, device_id_type=MESH)
+
+    @pl.when(has_down)
+    def _():
+        pl.semaphore_signal(barrier, inc=1, device_id=down, device_id_type=MESH)
+
+    pl.semaphore_wait(barrier, 2 + jnp.where(has_up, 1, 0) + jnp.where(has_down, 1, 0))
+
+    order = []
+    for t in range((lines + 1) // 2):
+        order += [t] if t == lines - 1 - t else [t, lines - 1 - t]
+    for t in order:
+        c_opp_x(t).start()
+        c_opp_y(t).start()
+    for t in order:
+        c_plain_x(t).start()
+        c_plain_y(t).start()
+
+    heads = head_ref[...]
+    heads_sq = dot_t(jnp.ones((8, heads.shape[1]), jnp.float32), heads * heads)[:1]
+    same = iota((n_head, n_head), 0) == iota((n_head, n_head), 1)
+    work[...] = head_gaussian(heads, heads, heads_sq) + jnp.where(same, ridge, 0.0)
+
+    def ring_sum(t):
+        c_opp_x(t).wait_recv()
+        to_y[t] = part_ref[t * PLANE + qy, :, lo] + opp_x[t]
+        c_sum_y(t).start()
+        c_opp_y(t).wait_recv()
+        to_x[t] = part_ref[t * PLANE + qx, :, hi] + opp_y[t]
+        c_sum_x(t).start()
+
+    def line_sum(t):
+        c_plain_x(t).wait_recv()
+        c_plain_y(t).wait_recv()
+        c_sum_x(t).wait_recv()
+        c_sum_y(t).wait_recv()
+        acc[t] = part_ref[t * PLANE + q] + from_x[t] + from_y[t]
+
+        @pl.when(has_down & (t >= line))
+        def _():
+            c_up(t).wait_recv()
+            acc[t] = acc[t] + from_down[t]
+
+        @pl.when(has_up & (t <= line))
+        def _():
+            c_down(t).wait_recv()
+            acc[t] = acc[t] + from_up[t]
+
+        @pl.when(t > line)
+        def _():
+            c_up(t).start()
+
+        @pl.when(t < line)
+        def _():
+            c_down(t).start()
+
+        @pl.when(t == line)
+        def _():
+            out_ref[...] = acc[t]
+
+    blocks = n_head // BLOCK
+
+    def some_blocks(a, b):
+        lax.fori_loop(a, b, lambda i, _: (eliminate(work, i, BLOCK), 0)[1], 0)
+
+    cuts = [blocks * i // (len(order) + 1) for i in range(len(order) + 2)]
+    some_blocks(cuts[0], cuts[1])
+    for t in order:
+        ring_sum(t)
+    for i, t in enumerate(order):
+        some_blocks(cuts[i + 1], cuts[i + 2])
+        line_sum(t)
+
+    head_row = iota((rows_here, n_head), 0)
+    head_col = iota((rows_here, n_head), 1)
+    block = head_col // pw
+    offset = head_row - block * quarter
+    hits = (offset >= 0) & (offset < quarter) & (head_col - block * pw == r * quarter + offset)
+    head_slab[...] = head_gaussian(emb_ref[...], heads, heads_sq) + jnp.where(hits, ridge, 0.0)
+
+    chunk = n_head
+
+    def land_chunk(i, _):
+        start = pl.multiple_of(i * chunk, chunk)
+        row = iota((chunk, n_head), 0) + start
+        hit = (row < pw) & (iota((chunk, n_head), 1) == c * pw + row)
+        land[pl.ds(start, chunk), :] = head_gaussian(
+            col_ref[pl.ds(start, chunk), :], heads, heads_sq
+        ) + jnp.where(hit, ridge, 0.0)
+        return 0
+
+    lax.fori_loop(0, half_cols // chunk, land_chunk, 0)
+
+    lower = iota((n_head, n_head), 1) // BLOCK <= iota((n_head, n_head), 0) // BLOCK
+    inverse = jnp.where(lower, work[...], 0.0)
+    panels = dot_t(head_slab[...], inverse)
+    panel_ref[...] = panels
+    for first in range(pw, half_cols, pw):
+        rows = dot_t(land[first : first + pw, :], inverse)
+        rem_ref[:, first - pw : first] = slab_ref[:, first : first + pw] - dot_t(panels, rows)
+
+    for t in range(lines):
+        for copy in (c_opp_x, c_opp_y, c_plain_x, c_plain_y, c_sum_x, c_sum_y):
+            copy(t).wait_send()
+
+        @pl.when(t > line)
+        def _(t=t):
+            c_up(t).wait_send()
+
+        @pl.when(t < line)
+        def _(t=t):
+            c_down(t).wait_send()
+
+
+def finish(ridge_shift, partial, embedded, column_emb, heads, kernel_slab, n_rows):
+    lines = n_rows // PLANE
+    _, share, wide = partial.shape
+    n_head = heads.shape[0]
+    rows_here = embedded.shape[0]
+    vmem = pl.BlockSpec(memory_space=pltpu.VMEM)
+    full = pltpu.VMEM((lines, share, wide), jnp.float32)
+    halved = pltpu.VMEM((lines, share, wide // 2), jnp.float32)
+    return pl.pallas_call(
+        finish_kernel,
+        out_shape=(
+            jax.ShapeDtypeStruct((share, wide), jnp.float32),
+            jax.ShapeDtypeStruct((rows_here, n_head), jnp.float32),
+            jax.ShapeDtypeStruct((rows_here, wide - PW), jnp.float32),
+        ),
+        in_specs=[pl.BlockSpec(memory_space=pltpu.SMEM)] + [vmem] * 5,
+        out_specs=(vmem,) * 3,
+        scratch_shapes=[
+            halved, halved, full, full, halved, halved, full, full, full,
+            pltpu.VMEM((n_head, n_head), jnp.float32),
+            pltpu.VMEM((wide, n_head), jnp.float32),
+            pltpu.VMEM((rows_here, n_head), jnp.float32),
+            pltpu.SemaphoreType.DMA((8, lines)),
+            pltpu.SemaphoreType.DMA((8, lines)),
+        ],
+        compiler_params=pltpu.CompilerParams(
+            collective_id=1, has_side_effects=True, vmem_limit_bytes=48 * 1024 * 1024
+        ),
+    )(ridge_shift, partial, embedded, column_emb, heads, kernel_slab)
+
+
 def per_device(points, landmark_index, targets, ridge_shift):
     rows_here = landmark_index.shape[0]
     block_points = points.shape[0]
@@ -217,46 +460,17 @@
     offset = row_ids - col_pos * quarter
     ridge_hits = (offset >= 0) & (offset < quarter) & (col_ids == row_pos * quarter + offset)
     kernel_slab = gaussian(embedded, column_emb) + jnp.where(ridge_hits, ridge, 0.0)
-    projected = lax.psum_scatter(
-        lax.dot_general(
-            all_targets,
-            kernel_slab,
-            (((0,), (0,)), ((), ())),
-            precision=exact_mode,
-            preferred_element_type=jnp.float32,
-        ),
-        "rows",
-        scatter_dimension=0,
-        tiled=True,
-    )
-
-    base = gaussian(heads, heads) + ridge * jnp.eye(2 * PW, dtype=jnp.float32)
-    inv0 = inverse_factor(base[:PW, :PW])
-    low = dot_t(base[PW:, :PW], inv0)
-    inv1 = inverse_factor(base[PW:, PW:] - dot_t(low, low))
-
-    hrow = lax.broadcasted_iota(jnp.int32, (rows_here, 2 * PW), 0)
-    hcol = lax.broadcasted_iota(jnp.int32, (rows_here, 2 * PW), 1)
-    hblock = hcol // PW
-    hoff = hrow - hblock * quarter
-    head_hits = (hoff >= 0) & (hoff < quarter) & (hcol - hblock * PW == row_pos * quarter + hoff)
-    head_slab = gaussian(embedded, heads) + jnp.where(head_hits, ridge, 0.0)
-
-    lrow = lax.broadcasted_iota(jnp.int32, (half_cols, 2 * PW), 0)
-    lcol = lax.broadcasted_iota(jnp.int32, (half_cols, 2 * PW), 1)
-    land_slab = gaussian(column_emb, heads) + jnp.where(
-        (lrow < PW) & (lcol == col_pos * PW + lrow), ridge, 0.0
-    )
-
-    def panels_of(slab):
-        first = dot_t(slab[:, :PW], inv0)
-        second = dot_t(slab[:, PW:] - dot_t(first, low), inv1)
-        return jnp.concatenate([first, second], axis=1)
-
-    panels = panels_of(head_slab)
-    land_panels = panels_of(land_slab)
-    remainder = kernel_slab[:, PW:] - dot_t(panels, land_panels[PW:])
-    return (projected, panels, remainder)
+    partial = lax.dot_general(
+        all_targets,
+        kernel_slab,
+        (((0,), (0,)), ((), ())),
+        precision=exact_mode,
+        preferred_element_type=jnp.float32,
+    )
+    share = partial.shape[0] // n_rows
+    return finish(
+        ridge_shift, partial.reshape(n_rows, share, half_cols), embedded, column_emb, heads, kernel_slab, n_rows
+    )
 
 
 def solution(mesh):

time: 157 us -> 141 us (0.90)
  the two profiles are of different devices: /device:TPU:0 before, /device:TPU:16 now
where the time goes in v3:
time: 141 us; the launch traced here: 140 us
  Pallas kernels  125 us (89%)
  matrix products  4.85 us (3%)
  local copies, waits for them, and re-layouts  4.61 us (3%)
  other arithmetic  3.9 us (3%)
  between operations  1.52 us (1%)
    pallas_call x1, Pallas kernels, finish(): pl.pallas_call(finish_kernel, out_shape=(jax.ShapeDtypeStruct((share, wid...  82.1 us
    pallas_call x1, Pallas kernels, gather(): pl.pallas_call(gather_kernel, out_shape=(jax.ShapeDtypeStruct((C // 2, wi...  43.3 us
    dot_general x1, matrix products, dot_t(): lax.dot_general(left, right, (((1,), (1,)), ((), ())), precision=exact_mo...  3 us

profile of v3, /device:TPU:16, one launch (start us, length us, event | category | flops | bytes accessed | tf_op | source)
XLA Modules:
  0.0 140.3 jit_solution(10752492503234817498)
XLA Ops:
  0.6 0.0 copy-start
  1.4 0.7 compare_and_fusion.1
  2.1 0.0 copy-done
  2.2 1.1 gather_fusion
  3.2 1.0 multiply_reduce_fusion.1
  4.3 0.0 copy-start.1
  4.3 43.3 %shard_map.67 = (f32[1024,768]{1,0:T(8,128)}, f32[2,128,768]{2,1,0:T(8,128)}, f32[2,256,256]{2,1,0:T(8,128)}) custom-call(f32[256,768]{1,0:T(8,128)} %get-tuple-element.10.emb_ref, f32[256,256]{1,0:T(8,128)} %tgt_ref.1), custom_call_target="tpu_custom_call" | custom-call | tf_op jit(solution)/shard_map/pallas_call | solution.py:178
  47.6 0.0 copy-start.3
  47.6 1.2 slice_bitcast_fusion.1
  48.9 2.2 %multiply_reduce_fusion = f32[1024]{0:T(1024)S(1)} fusion(f32[1024,768]{1,0:T(8,128)} %get-tuple-element.7.col_ref), kind=kLoop, calls=%fused_computation.1 | loop fusion | flops 1571840 | bytes 3149824 | tf_op jit(solution)/shard_map/reduce_sum | solution.py:23
  51.0 0.0 copy-done.1
  51.0 0.0 copy-done.3
  51.0 0.0 copy-start.2
  51.1 3.0 %fusion.4.slab_ref = f32[256,1024]{1,0:T(8,128)S(1)} fusion(f32[256,768]{1,0:T(8,128)S(1)} %copy-done.1, f32[1024,768]{1,0:T(8,128)S(1)} %copy-done.3, f32[]{:T(128)} %bitcast.10, s32[256]{0:T(256)S(1)} %fusion.10, f32[1024]{0:T(1024)S(1)} %multiply_reduce_fusion, f32[256]{0:T(256)S(1)} %get-tuple-element.9, pred[256]{0:T(512)(128)(4,1)S(1)} %compare_and_fusion), kind=kOutput, calls=%fused_computation.7 | convolution fusion | flops 2418278400 | bytes 4987140 | tf_op jit(solution)/shard_map/dot_general | solution.py:16
  54.1 1.8 %fusion.6 = f32[512,1024]{1,0:T(8,128)S(1)} fusion(f32[256,1024]{1,0:T(8,128)S(1)} %fusion.4.slab_ref, f32[256,256]{1,0:T(8,128)S(1)} %get-tuple-element.14, f32[256,256]{1,0:T(8,128)S(1)} %get-tuple-element.13), kind=kOutput, calls=%fused_computation.11 | convolution fusion | flops 1610743808 | bytes 3670016 | tf_op jit(solution)/shard_map/dot_general | solution.py:463
  55.9 0.0 copy-done.2
  55.9 82.1 %shard_map.68 = (f32[32,1024]{1,0:T(8,128)S(1)}, f32[256,256]{1,0:T(8,128)S(1)}, f32[256,896]{1,0:T(8,128)S(1)}) custom-call(f32[1]{0:T(128)} %copy.10.ridge_ref, f32[16,32,1024]{2,1,0:T(8,128)S(1)} %bitcast.11, f32[256,768]{1,0:T(8,128)S(1)} %copy-done.1, f32[1024,768]{1,0:T(8,128)} %get-tuple-element.7.col_ref, f32[256,768]{1,0:T(8,128)S(1)} %bitcast.12, ...), custom_call_target="tpu_custom_call" | custom-call | tf_op jit(solution)/shard_map/pallas_call | solution.py:420
  138.0 0.7 copy.11
  138.7 0.7 copy.12
  139.4 0.9 copy.13
  (3 shorter events, 0.0 us)
Async XLA Ops:
  0.6 1.5 %copy-start = (f32[512,768]{1,0:T(8,128)S(1)}, f32[512,768]{1,0:T(8,128)}, u32[]{:S(2)}) copy-start(f32[512,768]{1,0:T(8,128)} %param.4) | copy-start | bytes 4718596
  4.3 46.7 %copy-start.1 = (f32[256,768]{1,0:T(8,128)S(1)}, f32[256,768]{1,0:T(8,128)}, u32[]{:S(2)}) copy-start(f32[256,768]{1,0:T(8,128)} %get-tuple-element.10.emb_ref) | copy-start | bytes 2359300
  47.6 3.4 %copy-start.3 = (f32[1024,768]{1,0:T(8,128)S(1)}, f32[1024,768]{1,0:T(8,128)}, u32[]{:S(2)}) copy-start(f32[1024,768]{1,0:T(8,128)} %get-tuple-element.7.col_ref) | copy-start | bytes 9437188
  51.0 4.9 %copy-start.2 = (f32[2,128,768]{2,1,0:T(8,128)S(1)}, f32[2,128,768]{2,1,0:T(8,128)}, u32[]{:S(2)}) copy-start(f32[2,128,768]{2,1,0:T(8,128)} %get-tuple-element.8) | copy-start | bytes 2359300

commit v4 on v3

--- a/solution.py
+++ b/solution.py
@@ -326,47 +326,53 @@
         to_x[t] = part_ref[t * PLANE + qx, :, hi] + opp_y[t]
         c_sum_x(t).start()
 
-    def line_sum(t):
+    def ring_total(t):
         c_plain_x(t).wait_recv()
         c_plain_y(t).wait_recv()
         c_sum_x(t).wait_recv()
         c_sum_y(t).wait_recv()
         acc[t] = part_ref[t * PLANE + q] + from_x[t] + from_y[t]
 
-        @pl.when(has_down & (t >= line))
+    def line_step(step):
+        @pl.when(line <= step)
         def _():
-            c_up(t).wait_recv()
-            acc[t] = acc[t] + from_down[t]
-
-        @pl.when(has_up & (t <= line))
+            t = lines - 1 - step + line
+
+            @pl.when(has_down)
+            def _():
+                c_up(t).wait_recv()
+                acc[t] = acc[t] + from_down[t]
+
+            c_up(t).start()
+
+        @pl.when(lines - 1 - line <= step)
         def _():
-            c_down(t).wait_recv()
-            acc[t] = acc[t] + from_up[t]
-
-        @pl.when(t > line)
+            t = step - (lines - 1 - line)
+
+            @pl.when(has_up)
+            def _():
+                c_down(t).wait_recv()
+                acc[t] = acc[t] + from_up[t]
+
+            c_down(t).start()
+
+    def line_end():
+        out_ref[...] = acc[line]
+
+        @pl.when(has_down)
         def _():
-            c_up(t).start()
-
-        @pl.when(t < line)
+            c_up(line).wait_recv()
+            out_ref[...] += from_down[line]
+
+        @pl.when(has_up)
         def _():
-            c_down(t).start()
-
-        @pl.when(t == line)
-        def _():
-            out_ref[...] = acc[t]
+            c_down(line).wait_recv()
+            out_ref[...] += from_up[line]
 
     blocks = n_head // BLOCK
 
     def some_blocks(a, b):
         lax.fori_loop(a, b, lambda i, _: (eliminate(work, i, BLOCK), 0)[1], 0)
-
-    cuts = [blocks * i // (len(order) + 1) for i in range(len(order) + 2)]
-    some_blocks(cuts[0], cuts[1])
-    for t in order:
-        ring_sum(t)
-    for i, t in enumerate(order):
-        some_blocks(cuts[i + 1], cuts[i + 2])
-        line_sum(t)
 
     head_row = iota((rows_here, n_head), 0)
     head_col = iota((rows_here, n_head), 1)
@@ -388,6 +394,27 @@
 
     lax.fori_loop(0, half_cols // chunk, land_chunk, 0)
 
+    some_blocks(0, blocks // 8)
+    for t in order:
+        ring_sum(t)
+    some_blocks(blocks // 8, blocks * 3 // 8)
+    ring_total(order[0])
+    if lines > 1:
+        ring_total(order[1])
+    if lines > 1:
+        line_step(0)
+    some_blocks(blocks * 3 // 8, blocks // 2)
+    for t in order[2:]:
+        ring_total(t)
+    if lines > 2:
+        line_step(1)
+    some_blocks(blocks // 2, blocks * 5 // 8)
+    if lines > 3:
+        line_step(2)
+    some_blocks(blocks * 5 // 8, blocks)
+    for step in range(3, lines - 1):
+        line_step(step)
+
     lower = iota((n_head, n_head), 1) // BLOCK <= iota((n_head, n_head), 0) // BLOCK
     inverse = jnp.where(lower, work[...], 0.0)
     panels = dot_t(head_slab[...], inverse)
@@ -396,6 +423,7 @@
         rows = dot_t(land[first : first + pw, :], inverse)
         rem_ref[:, first - pw : first] = slab_ref[:, first : first + pw] - dot_t(panels, rows)
 
+    line_end()
     for t in range(lines):
         for copy in (c_opp_x, c_opp_y, c_plain_x, c_plain_y, c_sum_x, c_sum_y):
             copy(t).wait_send()

time: 141 us -> 104 us (0.74)
  the two profiles are of different devices: /device:TPU:16 before, /device:TPU:8 now
where the time goes in v4:
time: 104 us
  Pallas kernels  89.3 us (86%)
  matrix products  4.85 us (5%)
  local copies, waits for them, and re-layouts  4.61 us (4%)
  other arithmetic  3.9 us (4%)
  between operations  1.52 us (1%)
    pallas_call x1, Pallas kernels, finish(): pl.pallas_call(finish_kernel, out_shape=(jax.ShapeDtypeStruct((share, wid...  45.9 us
    pallas_call x1, Pallas kernels, gather(): pl.pallas_call(gather_kernel, out_shape=(jax.ShapeDtypeStruct((C // 2, wi...  43.3 us
    dot_general x1, matrix products, dot_t(): lax.dot_general(left, right, (((1,), (1,)), ((), ())), precision=exact_mo...  3 us
    unnamed x11, local copies, waits for them, and re-layouts  2.3 us
    reduce_sum x1, other arithmetic, gaussian(): right_sq = jnp.sum(right_rows * right_rows, axis=1)  2.16 us

profile of v4, /device:TPU:8, one launch (start us, length us, event | category | flops | bytes accessed | tf_op | source)
XLA Modules:
  0.0 104.1 jit_solution(6688487150849067019)
XLA Ops:
  0.6 0.0 copy-start
  1.4 0.7 compare_and_fusion.1
  2.1 0.0 copy-done
  2.2 1.1 %gather_fusion = f32[256,768]{1,0:T(8,128)S(1)} fusion(f32[512,768]{1,0:T(8,128)S(1)} %copy-done, s32[1024]{0:T(1024)S(1)} %pad_clamp_fusion), kind=kCustom, calls=%fused_computation | custom fusion | bytes 1573888 | tf_op jit(solution)/shard_map/jit(_take)/gather | solution.py:481
  3.2 1.0 multiply_reduce_fusion.1
  4.3 0.0 copy-start.1
  4.3 43.3 %shard_map.67 = (f32[1024,768]{1,0:T(8,128)}, f32[2,128,768]{2,1,0:T(8,128)}, f32[2,256,256]{2,1,0:T(8,128)}) custom-call(f32[256,768]{1,0:T(8,128)} %get-tuple-element.10.emb_ref, f32[256,256]{1,0:T(8,128)} %tgt_ref.1), custom_call_target="tpu_custom_call" | custom-call | tf_op jit(solution)/shard_map/pallas_call | solution.py:178
  47.6 0.0 copy-start.3
  47.6 1.2 %slice_bitcast_fusion.1 = (f32[256,256]{1,0:T(8,128)S(1)}, f32[256,256]{1,0:T(8,128)S(1)}) fusion(f32[2,256,256]{2,1,0:T(8,128)} %get-tuple-element.6), kind=kLoop, calls=%fused_computation.17 | loop fusion | bytes 1048576 | tf_op jit(solution)/shard_map/squeeze | solution.py:484
  48.8 2.2 %multiply_reduce_fusion = f32[1024]{0:T(1024)S(1)} fusion(f32[1024,768]{1,0:T(8,128)} %get-tuple-element.7.col_ref), kind=kLoop, calls=%fused_computation.1 | loop fusion | flops 1571840 | bytes 3149824 | tf_op jit(solution)/shard_map/reduce_sum | solution.py:23
  51.0 0.0 copy-done.1
  51.0 0.0 copy-done.3
  51.0 0.0 copy-start.2
  51.0 3.0 %fusion.4.slab_ref = f32[256,1024]{1,0:T(8,128)S(1)} fusion(f32[256,768]{1,0:T(8,128)S(1)} %copy-done.1, f32[1024,768]{1,0:T(8,128)S(1)} %copy-done.3, f32[]{:T(128)} %bitcast.10, s32[256]{0:T(256)S(1)} %fusion.10, f32[1024]{0:T(1024)S(1)} %multiply_reduce_fusion, f32[256]{0:T(256)S(1)} %get-tuple-element.9, pred[256]{0:T(512)(128)(4,1)S(1)} %compare_and_fusion), kind=kOutput, calls=%fused_computation.7 | convolution fusion | flops 2418278400 | bytes 4987140 | tf_op jit(solution)/shard_map/dot_general | solution.py:16
  54.1 1.8 %fusion.6 = f32[512,1024]{1,0:T(8,128)S(1)} fusion(f32[256,1024]{1,0:T(8,128)S(1)} %fusion.4.slab_ref, f32[256,256]{1,0:T(8,128)S(1)} %get-tuple-element.14, f32[256,256]{1,0:T(8,128)S(1)} %get-tuple-element.13), kind=kOutput, calls=%fused_computation.11 | convolution fusion | flops 1610743808 | bytes 3670016 | tf_op jit(solution)/shard_map/dot_general | solution.py:491
  55.9 0.0 copy-done.2
  55.9 45.9 %shard_map.68 = (f32[32,1024]{1,0:T(8,128)S(1)}, f32[256,256]{1,0:T(8,128)S(1)}, f32[256,896]{1,0:T(8,128)S(1)}) custom-call(f32[1]{0:T(128)} %copy.10.ridge_ref, f32[16,32,1024]{2,1,0:T(8,128)S(1)} %bitcast.11, f32[256,768]{1,0:T(8,128)S(1)} %copy-done.1, f32[1024,768]{1,0:T(8,128)} %get-tuple-element.7.col_ref, f32[256,768]{1,0:T(8,128)S(1)} %bitcast.12, ...), custom_call_target="tpu_custom_call" | custom-call | tf_op jit(solution)/shard_map/pallas_call | solution.py:448
  101.9 0.7 copy.11
  102.5 0.7 copy.12
  103.2 0.9 copy.13
  (3 shorter events, 0.0 us)
Async XLA Ops:
  0.6 1.5 %copy-start = (f32[512,768]{1,0:T(8,128)S(1)}, f32[512,768]{1,0:T(8,128)}, u32[]{:S(2)}) copy-start(f32[512,768]{1,0:T(8,128)} %param.4) | copy-start | bytes 4718596
  4.3 46.7 %copy-start.1 = (f32[256,768]{1,0:T(8,128)S(1)}, f32[256,768]{1,0:T(8,128)}, u32[]{:S(2)}) copy-start(f32[256,768]{1,0:T(8,128)} %get-tuple-element.10.emb_ref) | copy-start | bytes 2359300
  47.6 3.4 %copy-start.3 = (f32[1024,768]{1,0:T(8,128)S(1)}, f32[1024,768]{1,0:T(8,128)}, u32[]{:S(2)}) copy-start(f32[1024,768]{1,0:T(8,128)} %get-tuple-element.7.col_ref) | copy-start | bytes 9437188
  51.0 4.9 %copy-start.2 = (f32[2,128,768]{2,1,0:T(8,128)S(1)}, f32[2,128,768]{2,1,0:T(8,128)}, u32[]{:S(2)}) copy-start(f32[2,128,768]{2,1,0:T(8,128)} %get-tuple-element.8) | copy-start | bytes 2359300

commit v5 on v4

v5 whole, which is shorter than its diff:
```python
import jax
import jax.numpy as jnp
from jax import lax
from jax.experimental import pallas as pl
from jax.experimental.pallas import tpu as pltpu
from jax.sharding import PartitionSpec as P

C = 2048
PW = 128
BLOCK = 32

exact_mode = lax.Precision.HIGHEST


def dot_t(left, right):
    return lax.dot_general(
        left, right, (((1,), (1,)), ((), ())), precision=exact_mode, preferred_element_type=jnp.float32
    )


def gaussian(left_rows, right_rows):
    left_sq = jnp.sum(left_rows * left_rows, axis=1)
    right_sq = jnp.sum(right_rows * right_rows, axis=1)
    cross_term = dot_t(left_rows, right_rows)
    return jnp.exp(
        -(left_sq[:, None] + right_sq[None, :] - 2.0 * cross_term) / (2.0 * left_rows.shape[1])
    )


MESH = pl.DeviceIdType.MESH
PLANE = 4


def head_gaussian(left_rows, heads, heads_sq):
    left_sq = jnp.sum(left_rows * left_rows, axis=1, keepdims=True)
    return jnp.exp(
        -(left_sq + heads_sq - 2.0 * dot_t(left_rows, heads)) / (2.0 * left_rows.shape[1])
    )


def iota(shape, axis):
    return lax.broadcasted_iota(jnp.int32, shape, axis)


def eliminate(work, first, size):
    n = work.shape[0]
    start = pl.multiple_of(first * size, size)
    rows = work[pl.ds(start, size), :]
    rolled = pltpu.roll(rows, n - start, 1)
    lane = iota((size, 128), 1)
    row = iota((size, 128), 0)
    pair = jnp.where(lane < size, rolled[:, :128], jnp.where(lane == row + size, 1.0, 0.0))
    for j in range(0, size, 2):
        k = j + 1
        first_row, second_row = pair[j:k, :], pair[k : k + 1, :]
        a, b, d = pair[j:k, j:k], pair[j:k, k : k + 1], pair[k : k + 1, k : k + 1]
        scale = 1.0 / (a * d - b * b)
        left = (d * first_row - b * second_row) * scale
        right = (a * second_row - b * first_row) * scale
        later = row > k
        pair = (
            pair
            - jnp.where(later, pair[:, j:k], 0.0) * left
            - jnp.where(later, pair[:, k : k + 1], 0.0) * right
            - jnp.where(row == k, b / a, 0.0) * first_row
        )
    diagonal = jnp.sum(jnp.where(lane == row, pair, 0.0), axis=1, keepdims=True)
    block_inv = (pair / jnp.sqrt(diagonal))[:, size : 2 * size]

    wide_lane = iota((size, n), 1) - start
    inside = (wide_lane >= 0) & (wide_lane < size)
    eye = jnp.where(wide_lane == iota((size, n), 0), 1.0, 0.0)
    done = jnp.dot(
        block_inv, jnp.where(inside, eye, rows), precision=exact_mode, preferred_element_type=jnp.float32
    )
    below = jnp.where(wide_lane >= size, done, 0.0)
    update = lax.dot_general(
        below, done, (((0,), (0,)), ((), ())), precision=exact_mode, preferred_element_type=jnp.float32
    )
    all_row = iota((n, n), 0) - start
    all_lane = iota((n, n), 1) - start
    keep = jnp.where((all_row >= size) & (all_lane >= 0) & (all_lane < size), 0.0, work[...])
    work[...] = keep - update
    work[pl.ds(start, size), :] = done


def gather_kernel(
    ridge_ref, emb_ref, tgt_ref, col_ref, head_ref, all_tgt_ref, work, pair_ref, send, recv
):
    r = lax.axis_index("rows")
    c = lax.axis_index("cols")
    n_rows = lax.axis_size("rows")
    lines = n_rows // PLANE
    line, q = r // PLANE, r % PLANE
    quarter = col_ref.shape[0] // n_rows
    width = col_ref.shape[1]
    head_lines = pl.cdiv(PW, quarter * PLANE)
    x = line * PLANE + (q + 1 - 2 * (q % 2))
    y = line * PLANE + (q + 2) % PLANE
    qx, qy = q + 1 - 2 * (q % 2), (q + 2) % PLANE
    up, down = r + PLANE, r - PLANE
    has_up, has_down = line < lines - 1, line > 0
    core = (r, 1 - c)

    def rows_of(t, who):
        return pl.ds(pl.multiple_of((t * PLANE + who) * quarter, quarter), quarter)

    own = emb_ref.at[pl.ds(pl.multiple_of(c * quarter, quarter), quarter)]

    def remote(src, dst, kind, t, dev):
        return pltpu.make_async_remote_copy(
            src_ref=src, dst_ref=dst, send_sem=send.at[kind, t], recv_sem=recv.at[kind, t],
            device_id=dev, device_id_type=MESH,
        )

    def whole(kind, t, who, dev, first=False):
        dst = col_ref.at[rows_of(t, who)]
        return remote(own if first else dst, dst, kind, t, dev)

    def part(kind, t, who, side, dev, first=False):
        if quarter % 16 == 0:
            rows, cols = quarter // 2, width
        else:
            rows, cols = quarter, width // 2
        down_by, right_by = (side * rows, 0) if rows < quarter else (0, side * cols)
        start = pl.multiple_of((t * PLANE + who) * quarter + down_by, rows)
        dst = col_ref.at[pl.ds(start, rows), pl.ds(right_by, cols)]
        src = dst
        if first:
            start = pl.multiple_of(c * quarter + down_by, rows)
            src = emb_ref.at[pl.ds(start, rows), pl.ds(right_by, cols)]
        return remote(src, dst, kind, t, dev)

    barrier = pltpu.get_barrier_semaphore()
    for dev in ((x, c), (y, c), core):
        pl.semaphore_signal(barrier, inc=1, device_id=dev, device_id_type=MESH)

    @pl.when(has_up)
    def _():
        pl.semaphore_signal(barrier, inc=1, device_id=(up, c), device_id_type=MESH)

    @pl.when(has_down)
    def _():
        pl.semaphore_signal(barrier, inc=1, device_id=(down, c), device_id_type=MESH)

    pl.semaphore_wait(barrier, 3 + jnp.where(has_up, 1, 0) + jnp.where(has_down, 1, 0))

    def send_on(t, first=False):
        part(2, t, q, 0, (x, c), first).start()
        part(3, t, q, 1, (y, c), first).start()
        part(8, t, q, 1, (x, c), first).start()
        part(9, t, q, 0, (y, c), first).start()

    own_copy = pltpu.make_async_copy(own, col_ref.at[rows_of(line, q)], send.at[7, 0])
    tgt_cols = tgt_ref.shape[1]
    own_tgt = all_tgt_ref.at[:, pl.ds(pl.multiple_of(c * tgt_cols, tgt_cols), tgt_cols)]
    tgt_copy = pltpu.make_async_copy(tgt_ref, own_tgt, send.at[7, 1])

    @pl.when(has_up)
    def _():
        whole(0, line, q, (up, c), True).start()

    @pl.when(has_down)
    def _():
        whole(1, line, q, (down, c), True).start()

    send_on(line, True)
    own_copy.start()
    tgt_copy.start()
    tgt_swap = remote(tgt_ref, own_tgt, 6, 0, core)
    tgt_swap.start()

    def ring_stage(t):
        part(2, t, qx, 0, (x, c)).wait_recv()
        part(5, t, qx, 0, (y, c)).start()
        part(3, t, qy, 1, (y, c)).wait_recv()
        part(4, t, qy, 1, (x, c)).start()

    for step in range(1, lines + 1):
        if step < lines:
            @pl.when(line - step >= 0)
            def _(step=step):
                t = line - step
                whole(0, t, q, (up, c)).wait_recv()

                @pl.when(has_up)
                def _():
                    whole(0, t, q, (up, c)).start()

                send_on(t)

            @pl.when(line + step < lines)
            def _(step=step):
                t = line + step
                whole(1, t, q, (down, c)).wait_recv()

                @pl.when(has_down)
                def _():
                    whole(1, t, q, (down, c)).start()

                send_on(t)

        if step == 1:
            ring_stage(line)
        else:
            @pl.when(line - (step - 1) >= 0)
            def _(step=step):
                ring_stage(line - (step - 1))

            @pl.when(line + (step - 1) < lines)
            def _(step=step):
                ring_stage(line + (step - 1))

    opposite = PLANE - 1 - q

    def ring_rest(t):
        part(8, t, qx, 1, (x, c)).wait_recv()
        part(9, t, qy, 0, (y, c)).wait_recv()
        part(4, t, opposite, 1, (x, c)).wait_recv()
        part(5, t, opposite, 0, (y, c)).wait_recv()

    own_copy.wait()
    for t in range(head_lines):
        ring_rest(t)

    block_heads = col_ref.at[pl.ds(0, PW)]
    head_copy = pltpu.make_async_copy(block_heads, pair_ref.at[c], send.at[7, 2])
    head_swap = remote(block_heads, pair_ref.at[c], 6, 1, core)
    head_swap.start()
    head_copy.start()
    head_copy.wait()
    remote(block_heads, pair_ref.at[1 - c], 6, 1, core).wait()
    head_out = pltpu.make_async_copy(pair_ref, head_ref, send.at[7, 0])
    head_out.start()

    n_head = 2 * PW
    heads = pair_ref[...].reshape(n_head, width)
    heads_sq = dot_t(jnp.ones((8, width), jnp.float32), heads * heads)[:1]
    same = iota((n_head, n_head), 0) == iota((n_head, n_head), 1)
    work[...] = head_gaussian(heads, heads, heads_sq) + jnp.where(same, ridge_ref[0], 0.0)
    lax.fori_loop(0, n_head // BLOCK, lambda i, _: (eliminate(work, i, BLOCK), 0)[1], 0)
    lower = iota((n_head, n_head), 1) // BLOCK <= iota((n_head, n_head), 0) // BLOCK
    work[...] = jnp.where(lower, work[...], 0.0)

    for t in range(head_lines, lines):
        ring_rest(t)

    for t in range(lines):
        part(2, t, q, 0, (x, c)).wait_send()
        part(3, t, q, 1, (y, c)).wait_send()
        part(8, t, q, 1, (x, c)).wait_send()
        part(9, t, q, 0, (y, c)).wait_send()
        part(4, t, qy, 1, (x, c)).wait_send()
        part(5, t, qx, 0, (y, c)).wait_send()

        @pl.when(has_up & (t <= line))
        def _(t=t):
            whole(0, t, q, (up, c)).wait_send()

        @pl.when(has_down & (t >= line))
        def _(t=t):
            whole(1, t, q, (down, c)).wait_send()

    tgt_copy.wait()
    head_out.wait()
    other_tgt = all_tgt_ref.at[:, pl.ds(pl.multiple_of((1 - c) * tgt_cols, tgt_cols), tgt_cols)]
    remote(tgt_ref, other_tgt, 6, 0, core).wait()


def gather(ridge_shift, embedded, targets, n_rows):
    width = embedded.shape[1]
    hbm = pl.BlockSpec(memory_space=pl.ANY)
    kinds = (10, max(n_rows // PLANE, 3))
    return pl.pallas_call(
        gather_kernel,
        out_shape=(
            jax.ShapeDtypeStruct((C // 2, width), jnp.float32),
            jax.ShapeDtypeStruct((2, PW, width), jnp.float32),
            jax.ShapeDtypeStruct((targets.shape[0], 2 * targets.shape[1]), jnp.float32),
            jax.ShapeDtypeStruct((2 * PW, 2 * PW), jnp.float32),
        ),
        in_specs=[pl.BlockSpec(memory_space=pltpu.SMEM), hbm, hbm],
        out_specs=(hbm, hbm, hbm, pl.BlockSpec(memory_space=pltpu.VMEM)),
        scratch_shapes=[
            pltpu.VMEM((2, PW, width), jnp.float32),
            pltpu.SemaphoreType.DMA(kinds),
            pltpu.SemaphoreType.DMA(kinds),
        ],
        compiler_params=pltpu.CompilerParams(
            collective_id=0, has_side_effects=True, vmem_limit_bytes=48 * 1024 * 1024
        ),
    )(ridge_shift, embedded, targets)


def finish_kernel(
    ridge_ref, part_ref, emb_ref, col_ref, head_ref, slab_ref, inv_ref, out_ref, panel_ref, rem_ref,
    opp_x, opp_y, from_x, from_y, to_x, to_y, acc, from_down, from_up, land, head_slab, send, recv,
):
    r = lax.axis_index("rows")
    c = lax.axis_index("cols")
    n_rows = lax.axis_size("rows")
    lines = n_rows // PLANE
    line, q = r // PLANE, r % PLANE
    qx, qy = q + 1 - 2 * (q % 2), (q + 2) % PLANE
    opposite = PLANE - 1 - q
    x, y = (line * PLANE + qx, c), (line * PLANE + qy, c)
    up, down = (r + PLANE, c), (r - PLANE, c)
    has_up, has_down = line < lines - 1, line > 0
    wide = part_ref.shape[2]
    half = wide // 2
    lo, hi = pl.ds(0, half), pl.ds(half, half)
    rows_here = emb_ref.shape[0]
    half_cols = col_ref.shape[0]
    quarter = half_cols // n_rows
    n_head = head_ref.shape[0]
    pw = n_head // 2
    ridge = ridge_ref[0]

    def remote(src, dst, kind, t, dev):
        return pltpu.make_async_remote_copy(
            src_ref=src, dst_ref=dst, send_sem=send.at[kind, t], recv_sem=recv.at[kind, t],
            device_id=dev, device_id_type=MESH,
        )

    def c_opp_x(t):
        return remote(part_ref.at[t * PLANE + opposite, :, lo], opp_x.at[t], 0, t, x)

    def c_opp_y(t):
        return remote(part_ref.at[t * PLANE + opposite, :, hi], opp_y.at[t], 1, t, y)

    def c_plain_x(t):
        return remote(part_ref.at[t * PLANE + qx, :, lo], from_x.at[t, :, lo], 2, t, x)

    def c_plain_y(t):
        return remote(part_ref.at[t * PLANE + qy, :, hi], from_y.at[t, :, hi], 3, t, y)

    def c_sum_x(t):
        return remote(to_x.at[t], from_x.at[t, :, hi], 4, t, x)

    def c_sum_y(t):
        return remote(to_y.at[t], from_y.at[t, :, lo], 5, t, y)

    def c_up(t):
        return remote(acc.at[t], from_down.at[t], 6, t, up)

    def c_down(t):
        return remote(acc.at[t], from_up.at[t], 7, t, down)

    barrier = pltpu.get_barrier_semaphore()
    for dev in (x, y):
        pl.semaphore_signal(barrier, inc=1, device_id=dev, device_id_type=MESH)

    @pl.when(has_up)
    def _():
        pl.semaphore_signal(barrier, inc=1, device_id=up, device_id_type=MESH)

    @pl.when(has_down)
    def _():
        pl.semaphore_signal(barrier, inc=1, device_id=down, device_id_type=MESH)

    pl.semaphore_wait(barrier, 2 + jnp.where(has_up, 1, 0) + jnp.where(has_down, 1, 0))

    order = []
    for t in range((lines + 1) // 2):
        order += [t] if t == lines - 1 - t else [t, lines - 1 - t]
    for t in order:
        c_opp_x(t).start()
        c_opp_y(t).start()
    for t in order:
        c_plain_x(t).start()
        c_plain_y(t).start()

    heads = head_ref[...]
    heads_sq = dot_t(jnp.ones((8, heads.shape[1]), jnp.float32), heads * heads)[:1]
    def ring_sum(t):
        c_opp_x(t).wait_recv()
        to_y[t] = part_ref[t * PLANE + qy, :, lo] + opp_x[t]
        c_sum_y(t).start()
        c_opp_y(t).wait_recv()
        to_x[t] = part_ref[t * PLANE + qx, :, hi] + opp_y[t]
        c_sum_x(t).start()

    def ring_total(t):
        c_plain_x(t).wait_recv()
        c_plain_y(t).wait_recv()
        c_sum_x(t).wait_recv()
        c_sum_y(t).wait_recv()
        acc[t] = part_ref[t * PLANE + q] + from_x[t] + from_y[t]

    def line_step(step):
        @pl.when(line <= step)
        def _():
            t = lines - 1 - step + line

            @pl.when(has_down)
            def _():
                c_up(t).wait_recv()
                acc[t] = acc[t] + from_down[t]

            c_up(t).start()

        @pl.when(lines - 1 - line <= step)
        def _():
            t = step - (lines - 1 - line)

            @pl.when(has_up)
            def _():
                c_down(t).wait_recv()
                acc[t] = acc[t] + from_up[t]

            c_down(t).start()

    def line_end():
        out_ref[...] = acc[line]

        @pl.when(has_down)
        def _():
            c_up(line).wait_recv()
            out_ref[...] += from_down[line]

        @pl.when(has_up)
        def _():
            c_down(line).wait_recv()
            out_ref[...] += from_up[line]

    head_row = iota((rows_here, n_head), 0)
    head_col = iota((rows_here, n_head), 1)
    block = head_col // pw
    offset = head_row - block * quarter
    hits = (offset >= 0) & (offset < quarter) & (head_col - block * pw == r * quarter + offset)
    head_slab[...] = head_gaussian(emb_ref[...], heads, heads_sq) + jnp.where(hits, ridge, 0.0)

    chunk = n_head

    def land_chunk(i, _):
        start = pl.multiple_of(i * chunk, chunk)
        row = iota((chunk, n_head), 0) + start
        hit = (row < pw) & (iota((chunk, n_head), 1) == c * pw + row)
        land[pl.ds(start, chunk), :] = head_gaussian(
            col_ref[pl.ds(start, chunk), :], heads, heads_sq
        ) + jnp.where(hit, ridge, 0.0)
        return 0

    lax.fori_loop(0, half_cols // chunk, land_chunk, 0)

    for t in order:
        ring_sum(t)
    inverse = inv_ref[...]
    panels = dot_t(head_slab[...], inverse)
    panel_ref[...] = panels

    def remainder(first):
        rows = dot_t(land[first : first + pw, :], inverse)
        rem_ref[:, first - pw : first] = slab_ref[:, first : first + pw] - dot_t(panels, rows)

    firsts = list(range(pw, half_cols, pw))
    ring_total(order[0])
    if lines > 1:
        ring_total(order[1])
        line_step(0)
    for first in firsts[:2]:
        remainder(first)
    for t in order[2:]:
        ring_total(t)
    if lines > 2:
        line_step(1)
    for first in firsts[2:4]:
        remainder(first)
    if lines > 3:
        line_step(2)
    for first in firsts[4:]:
        remainder(first)
    for step in range(3, lines - 1):
        line_step(step)
    line_end()
    for t in range(lines):
        for copy in (c_opp_x, c_opp_y, c_plain_x, c_plain_y, c_sum_x, c_sum_y):
            copy(t).wait_send()

        @pl.when(t > line)
        def _(t=t):
            c_up(t).wait_send()

        @pl.when(t < line)
        def _(t=t):
            c_down(t).wait_send()


def finish(ridge_shift, partial, embedded, column_emb, heads, kernel_slab, inverse, n_rows):
    lines = n_rows // PLANE
    _, share, wide = partial.shape
    n_head = heads.shape[0]
    rows_here = embedded.shape[0]
    vmem = pl.BlockSpec(memory_space=pltpu.VMEM)
    full = pltpu.VMEM((lines, share, wide), jnp.float32)
    halved = pltpu.VMEM((lines, share, wide // 2), jnp.float32)
    return pl.pallas_call(
        finish_kernel,
        out_shape=(
            jax.ShapeDtypeStruct((share, wide), jnp.float32),
            jax.ShapeDtypeStruct((rows_here, n_head), jnp.float32),
            jax.ShapeDtypeStruct((rows_here, wide - PW), jnp.float32),
        ),
        in_specs=[pl.BlockSpec(memory_space=pltpu.SMEM)] + [vmem] * 6,
        out_specs=(vmem,) * 3,
        scratch_shapes=[
            halved, halved, full, full, halved, halved, full, full, full,
            pltpu.VMEM((wide, n_head), jnp.float32),
            pltpu.VMEM((rows_here, n_head), jnp.float32),
            pltpu.SemaphoreType.DMA((8, lines)),
            pltpu.SemaphoreType.DMA((8, lines)),
        ],
        compiler_params=pltpu.CompilerParams(
            collective_id=1, has_side_effects=True, vmem_limit_bytes=48 * 1024 * 1024
        ),
    )(ridge_shift, partial, embedded, column_emb, heads, kernel_slab, inverse)


def per_device(points, landmark_index, targets, ridge_shift):
    rows_here = landmark_index.shape[0]
    block_points = points.shape[0]
    row_pos = lax.axis_index("rows")
    col_pos = lax.axis_index("cols")
    n_rows = lax.axis_size("rows")
    half_cols = C // 2
    quarter = half_cols // n_rows
    ridge = ridge_shift[0]
    local_index = landmark_index - row_pos * block_points
    embedded = jnp.take(points, local_index, axis=0)
    column_emb, head_pair, all_targets, inverse = gather(ridge_shift, embedded, targets, n_rows)
    heads = head_pair.reshape(2 * PW, -1)

    row_ids = lax.broadcasted_iota(jnp.int32, (rows_here, half_cols), 0)
    col_ids = lax.broadcasted_iota(jnp.int32, (rows_here, half_cols), 1)
    offset = row_ids - col_pos * quarter
    ridge_hits = (offset >= 0) & (offset < quarter) & (col_ids == row_pos * quarter + offset)
    kernel_slab = gaussian(embedded, column_emb) + jnp.where(ridge_hits, ridge, 0.0)
    partial = lax.dot_general(
        all_targets,
        kernel_slab,
        (((0,), (0,)), ((), ())),
        precision=exact_mode,
        preferred_element_type=jnp.float32,
    )
    share = partial.shape[0] // n_rows
    parts = partial.reshape(n_rows, share, half_cols)
    return finish(ridge_shift, parts, embedded, column_emb, heads, kernel_slab, inverse, n_rows)


def solution(mesh):
    in_specs = (P("rows", None), P("rows"), P("rows", "cols"), P())
    out_specs = (P("rows", "cols"), P("rows", None), P("rows", "cols"))
    return jax.shard_map(
        per_device, mesh=mesh, in_specs=in_specs, out_specs=out_specs, check_vma=False
    )
```

time: 104 us -> 111 us (1.067)
  the two profiles are of different devices: /device:TPU:8 before, /device:TPU:0 now
where the time goes in v5:
time: 111 us
  Pallas kernels  98.7 us (89%)
  matrix products  6.22 us (6%)
  local copies, waits for them, and re-layouts  3.39 us (3%)
  between operations  1.49 us (1%)
  other arithmetic  1.22 us (1%)
    pallas_call x1, Pallas kernels, gather(): pl.pallas_call(gather_kernel, out_shape=(jax.ShapeDtypeStruct((C // 2, wi...  59.9 us
    pallas_call x1, Pallas kernels, finish(): pl.pallas_call(finish_kernel, out_shape=(jax.ShapeDtypeStruct((share, wid...  38.8 us
    dot_general x1, matrix products, per_device(): lax.dot_general(all_targets, kernel_slab, (((0,), (0,)), ((), ())), preci...  3.21 us
    dot_general x1, matrix products, dot_t(): lax.dot_general(left, right, (((1,), (1,)), ((), ())), precision=exact_mo...  3 us
    unnamed x9, local copies, waits for them, and re-layouts  2.3 us

profile of v5, /device:TPU:0, one launch (start us, length us, event | category | flops | bytes accessed | tf_op | source)
XLA Modules:
  0.0 111.0 jit_solution(7674392393960882781)
XLA Ops:
  0.6 0.0 copy-start
  1.4 0.7 compare_and_fusion.1
  2.1 0.0 copy-done
  2.2 0.0 copy-start.2
  2.2 1.1 gather_fusion
  3.3 0.2 multiply_reduce_fusion.1
  3.5 0.0 copy-done.2
  3.5 59.9 %shard_map.67 = (f32[1024,768]{1,0:T(8,128)S(1)}, f32[2,128,768]{2,1,0:T(8,128)S(1)}, f32[256,512]{1,0:T(8,128)S(1)}, f32[256,256]{1,0:T(8,128)S(1)}) custom-call(f32[1]{0:T(128)} %copy.10.ridge_ref, f32[256,768]{1,0:T(8,128)S(1)} %get-tuple-element.12.emb_ref, f32[256,256]{1,0:T(8,128)S(1)} %copy-done.2), custom_call_target="tpu_custom_call" | custom-call | tf_op jit(solution)/shard_map/pallas_call | solution.py:274
  63.4 0.0 copy-start.1
  63.5 0.3 multiply_reduce_fusion
  63.7 3.0 %fusion.4.slab_ref = f32[256,1024]{1,0:T(8,128)S(1)} fusion(f32[256,768]{1,0:T(8,128)S(1)} %get-tuple-element.12.emb_ref, f32[1024,768]{1,0:T(8,128)S(1)} %get-tuple-element.8.col_ref, f32[]{:T(128)} %bitcast.7, s32[256]{0:T(256)S(1)} %fusion.6, f32[1024]{0:T(1024)S(1)} %multiply_reduce_fusion, f32[256]{0:T(256)S(1)} %get-tuple-element.11, ...), kind=kOutput, calls=%fused_computation.7 | convolution fusion | flops 2418278400 | bytes 4987140 | tf_op jit(solution)/shard_map/dot_general | solution.py:16
  66.7 0.0 copy-done.1
  66.7 3.2 %fusion.7 = f32[512,1024]{1,0:T(8,128)} fusion(f32[256,512]{1,0:T(8,128)S(1)} %get-tuple-element.7, f32[256,1024]{1,0:T(8,128)S(1)} %fusion.4.slab_ref), kind=kOutput, calls=%fused_computation.18 | convolution fusion | flops 1610612736 | bytes 3670016 | tf_op jit(solution)/shard_map/dot_general | solution.py:538
  70.0 38.8 %shard_map.68 = (f32[32,1024]{1,0:T(8,128)S(1)}, f32[256,256]{1,0:T(8,128)S(1)}, f32[256,896]{1,0:T(8,128)S(1)}) custom-call(f32[1]{0:T(128)} %copy.10.ridge_ref, f32[16,32,1024]{2,1,0:T(8,128)} %bitcast.9, f32[256,768]{1,0:T(8,128)S(1)} %get-tuple-element.12.emb_ref, f32[1024,768]{1,0:T(8,128)} %copy-done.1, f32[256,768]{1,0:T(8,128)S(1)} %bitcast.8, ...), custom_call_target="tpu_custom_call" | custom-call | tf_op jit(solution)/shard_map/pallas_call | solution.py:497
  108.8 0.7 copy.11
  109.4 0.7 copy.12
  110.1 0.9 copy.13
  (3 shorter events, 0.0 us)
Async XLA Ops:
  0.6 1.5 %copy-start = (f32[512,768]{1,0:T(8,128)S(1)}, f32[512,768]{1,0:T(8,128)}, u32[]{:S(2)}) copy-start(f32[512,768]{1,0:T(8,128)} %param.4) | copy-start | bytes 4718596
  2.2 1.3 %copy-start.2 = (f32[256,256]{1,0:T(8,128)S(1)}, f32[256,256]{1,0:T(8,128)}, u32[]{:S(2)}) copy-start(f32[256,256]{1,0:T(8,128)} %tgt_ref.1) | copy-start | bytes 786436
  63.4 3.3 %copy-start.1 = (f32[1024,768]{1,0:T(8,128)}, f32[1024,768]{1,0:T(8,128)S(1)}, u32[]{:S(2)}) copy-start(f32[1024,768]{1,0:T(8,128)S(1)} %get-tuple-element.8.col_ref) | copy-start | bytes 9437188

commit v6 on v5

--- a/solution.py
+++ b/solution.py
@@ -85,7 +85,7 @@
 
 
 def gather_kernel(
-    ridge_ref, emb_ref, tgt_ref, col_ref, head_ref, all_tgt_ref, work, pair_ref, send, recv
+    emb_ref, tgt_ref, col_ref, head_ref, all_tgt_ref, send, recv
 ):
     r = lax.axis_index("rows")
     c = lax.axis_index("cols")
@@ -224,23 +224,10 @@
         ring_rest(t)
 
     block_heads = col_ref.at[pl.ds(0, PW)]
-    head_copy = pltpu.make_async_copy(block_heads, pair_ref.at[c], send.at[7, 2])
-    head_swap = remote(block_heads, pair_ref.at[c], 6, 1, core)
+    head_copy = pltpu.make_async_copy(block_heads, head_ref.at[c], send.at[7, 2])
+    head_swap = remote(block_heads, head_ref.at[c], 6, 1, core)
     head_swap.start()
     head_copy.start()
-    head_copy.wait()
-    remote(block_heads, pair_ref.at[1 - c], 6, 1, core).wait()
-    head_out = pltpu.make_async_copy(pair_ref, head_ref, send.at[7, 0])
-    head_out.start()
-
-    n_head = 2 * PW
-    heads = pair_ref[...].reshape(n_head, width)
-    heads_sq = dot_t(jnp.ones((8, width), jnp.float32), heads * heads)[:1]
-    same = iota((n_head, n_head), 0) == iota((n_head, n_head), 1)
-    work[...] = head_gaussian(heads, heads, heads_sq) + jnp.where(same, ridge_ref[0], 0.0)
-    lax.fori_loop(0, n_head // BLOCK, lambda i, _: (eliminate(work, i, BLOCK), 0)[1], 0)
-    lower = iota((n_head, n_head), 1) // BLOCK <= iota((n_head, n_head), 0) // BLOCK
-    work[...] = jnp.where(lower, work[...], 0.0)
 
     for t in range(head_lines, lines):
         ring_rest(t)
@@ -262,12 +249,13 @@
             whole(1, t, q, (down, c)).wait_send()
 
     tgt_copy.wait()
-    head_out.wait()
+    head_copy.wait()
+    remote(block_heads, head_ref.at[1 - c], 6, 1, core).wait()
     other_tgt = all_tgt_ref.at[:, pl.ds(pl.multiple_of((1 - c) * tgt_cols, tgt_cols), tgt_cols)]
     remote(tgt_ref, other_tgt, 6, 0, core).wait()
 
 
-def gather(ridge_shift, embedded, targets, n_rows):
+def gather(embedded, targets, n_rows):
     width = embedded.shape[1]
     hbm = pl.BlockSpec(memory_space=pl.ANY)
     kinds = (10, max(n_rows // PLANE, 3))
@@ -277,24 +265,20 @@
             jax.ShapeDtypeStruct((C // 2, width), jnp.float32),
             jax.ShapeDtypeStruct((2, PW, width), jnp.float32),
             jax.ShapeDtypeStruct((targets.shape[0], 2 * targets.shape[1]), jnp.float32),
-            jax.ShapeDtypeStruct((2 * PW, 2 * PW), jnp.float32),
         ),
-        in_specs=[pl.BlockSpec(memory_space=pltpu.SMEM), hbm, hbm],
-        out_specs=(hbm, hbm, hbm, pl.BlockSpec(memory_space=pltpu.VMEM)),
+        in_specs=[hbm, hbm],
+        out_specs=(hbm, hbm, hbm),
         scratch_shapes=[
-            pltpu.VMEM((2, PW, width), jnp.float32),
             pltpu.SemaphoreType.DMA(kinds),
             pltpu.SemaphoreType.DMA(kinds),
         ],
-        compiler_params=pltpu.CompilerParams(
-            collective_id=0, has_side_effects=True, vmem_limit_bytes=48 * 1024 * 1024
-        ),
-    )(ridge_shift, embedded, targets)
+        compiler_params=pltpu.CompilerParams(collective_id=0, has_side_effects=True),
+    )(embedded, targets)
 
 
 def finish_kernel(
-    ridge_ref, part_ref, emb_ref, col_ref, head_ref, slab_ref, inv_ref, out_ref, panel_ref, rem_ref,
-    opp_x, opp_y, from_x, from_y, to_x, to_y, acc, from_down, from_up, land, head_slab, send, recv,
+    ridge_ref, part_ref, emb_ref, col_ref, head_ref, slab_ref, out_ref, panel_ref, rem_ref,
+    opp_x, opp_y, from_x, from_y, to_x, to_y, acc, from_down, from_up, work, land, head_slab, send, recv,
 ):
     r = lax.axis_index("rows")
     c = lax.axis_index("cols")
@@ -363,15 +347,27 @@
     order = []
     for t in range((lines + 1) // 2):
         order += [t] if t == lines - 1 - t else [t, lines - 1 - t]
-    for t in order:
-        c_opp_x(t).start()
-        c_opp_y(t).start()
-    for t in order:
-        c_plain_x(t).start()
-        c_plain_y(t).start()
+    def ring_start(shards):
+        for t in shards:
+            c_opp_x(t).start()
+            c_opp_y(t).start()
+        for t in shards:
+            c_plain_x(t).start()
+            c_plain_y(t).start()
+
+    ends, middle = order[:2], order[2:]
+    ring_start(ends)
 
     heads = head_ref[...]
     heads_sq = dot_t(jnp.ones((8, heads.shape[1]), jnp.float32), heads * heads)[:1]
+    same = iota((n_head, n_head), 0) == iota((n_head, n_head), 1)
+    work[...] = head_gaussian(heads, heads, heads_sq) + jnp.where(same, ridge, 0.0)
+    blocks = n_head // BLOCK
+
+    def factor(first, last):
+        step = lambda i, _: (eliminate(work, i, BLOCK), 0)[1]
+        lax.fori_loop(blocks * first // 8, blocks * last // 8, step, 0)
+
     def ring_sum(t):
         c_opp_x(t).wait_recv()
         to_y[t] = part_ref[t * PLANE + qy, :, lo] + opp_x[t]
@@ -441,37 +437,36 @@
         ) + jnp.where(hit, ridge, 0.0)
         return 0
 
-    lax.fori_loop(0, half_cols // chunk, land_chunk, 0)
-
-    for t in order:
+
+    for t in ends:
         ring_sum(t)
-    inverse = inv_ref[...]
-    panels = dot_t(head_slab[...], inverse)
-    panel_ref[...] = panels
-
-    def remainder(first):
-        rows = dot_t(land[first : first + pw, :], inverse)
-        rem_ref[:, first - pw : first] = slab_ref[:, first : first + pw] - dot_t(panels, rows)
-
-    firsts = list(range(pw, half_cols, pw))
-    ring_total(order[0])
+    ring_start(middle)
+    factor(0, 2)
+    for t in middle:
+        ring_sum(t)
+    for t in ends:
+        ring_total(t)
     if lines > 1:
-        ring_total(order[1])
         line_step(0)
-    for first in firsts[:2]:
-        remainder(first)
-    for t in order[2:]:
+    factor(2, 4)
+    for t in middle:
         ring_total(t)
     if lines > 2:
         line_step(1)
-    for first in firsts[2:4]:
-        remainder(first)
+    factor(4, 6)
     if lines > 3:
         line_step(2)
-    for first in firsts[4:]:
-        remainder(first)
+    factor(6, 8)
     for step in range(3, lines - 1):
         line_step(step)
+    lax.fori_loop(0, half_cols // chunk, land_chunk, 0)
+    lower = iota((n_head, n_head), 1) // BLOCK <= iota((n_head, n_head), 0) // BLOCK
+    inverse = jnp.where(lower, work[...], 0.0)
+    panels = dot_t(head_slab[...], inverse)
+    panel_ref[...] = panels
+    for first in range(pw, half_cols, pw):
+        rows = dot_t(land[first : first + pw, :], inverse)
+        rem_ref[:, first - pw : first] = slab_ref[:, first : first + pw] - dot_t(panels, rows)
     line_end()
     for t in range(lines):
         for copy in (c_opp_x, c_opp_y, c_plain_x, c_plain_y, c_sum_x, c_sum_y):
@@ -486,7 +481,7 @@
             c_down(t).wait_send()
 
 
-def finish(ridge_shift, partial, embedded, column_emb, heads, kernel_slab, inverse, n_rows):
+def finish(ridge_shift, partial, embedded, column_emb, heads, kernel_slab, n_rows):
     lines = n_rows // PLANE
     _, share, wide = partial.shape
     n_head = heads.shape[0]
@@ -501,10 +496,11 @@
             jax.ShapeDtypeStruct((rows_here, n_head), jnp.float32),
             jax.ShapeDtypeStruct((rows_here, wide - PW), jnp.float32),
         ),
-        in_specs=[pl.BlockSpec(memory_space=pltpu.SMEM)] + [vmem] * 6,
+        in_specs=[pl.BlockSpec(memory_space=pltpu.SMEM)] + [vmem] * 5,
         out_specs=(vmem,) * 3,
         scratch_shapes=[
             halved, halved, full, full, halved, halved, full, full, full,
+            pltpu.VMEM((n_head, n_head), jnp.float32),
             pltpu.VMEM((wide, n_head), jnp.float32),
             pltpu.VMEM((rows_here, n_head), jnp.float32),
             pltpu.SemaphoreType.DMA((8, lines)),
@@ -513,7 +509,7 @@
         compiler_params=pltpu.CompilerParams(
             collective_id=1, has_side_effects=True, vmem_limit_bytes=48 * 1024 * 1024
         ),
-    )(ridge_shift, partial, embedded, column_emb, heads, kernel_slab, inverse)
+    )(ridge_shift, partial, embedded, column_emb, heads, kernel_slab)
 
 
 def per_device(points, landmark_index, targets, ridge_shift):
@@ -527,7 +523,7 @@
     ridge = ridge_shift[0]
     local_index = landmark_index - row_pos * block_points
     embedded = jnp.take(points, local_index, axis=0)
-    column_emb, head_pair, all_targets, inverse = gather(ridge_shift, embedded, targets, n_rows)
+    column_emb, head_pair, all_targets = gather(embedded, targets, n_rows)
     heads = head_pair.reshape(2 * PW, -1)
 
     row_ids = lax.broadcasted_iota(jnp.int32, (rows_here, half_cols), 0)
@@ -544,7 +540,7 @@
     )
     share = partial.shape[0] // n_rows
     parts = partial.reshape(n_rows, share, half_cols)
-    return finish(ridge_shift, parts, embedded, column_emb, heads, kernel_slab, inverse, n_rows)
+    return finish(ridge_shift, parts, embedded, column_emb, heads, kernel_slab, n_rows)
 
 
 def solution(mesh):

time: 111 us -> 106 us (0.955)
  the two profiles are of different devices: /device:TPU:0 before, /device:TPU:8 now
where the time goes in v6:
time: 106 us
  Pallas kernels  91.8 us (87%)
  matrix products  4.85 us (5%)
  other arithmetic  4.05 us (4%)
  local copies, waits for them, and re-layouts  3.89 us (4%)
  between operations  1.51 us (1%)
    pallas_call x1, Pallas kernels, finish(): pl.pallas_call(finish_kernel, out_shape=(jax.ShapeDtypeStruct((share, wid...  50.8 us
    pallas_call x1, Pallas kernels, gather(): pl.pallas_call(gather_kernel, out_shape=(jax.ShapeDtypeStruct((C // 2, wi...  41 us
    dot_general x1, matrix products, dot_t(): lax.dot_general(left, right, (((1,), (1,)), ((), ())), precision=exact_mo...  3 us
    unnamed x13, local copies, waits for them, and re-layouts  2.8 us
    reduce_sum x1, other arithmetic, gaussian(): right_sq = jnp.sum(right_rows * right_rows, axis=1)  2.31 us

profile of v6, /device:TPU:8, one launch (start us, length us, event | category | flops | bytes accessed | tf_op | source)
XLA Modules:
  0.0 106.1 jit_solution(2773456583147679489)
XLA Ops:
  0.6 0.0 copy-start
  1.4 0.7 compare_and_fusion.1
  2.1 0.0 copy-done
  2.2 1.1 %gather_fusion = f32[256,768]{1,0:T(8,128)S(1)} fusion(f32[512,768]{1,0:T(8,128)S(1)} %copy-done, s32[1024]{0:T(1024)S(1)} %pad_clamp_fusion), kind=kCustom, calls=%fused_computation | custom fusion | bytes 1573888 | tf_op jit(solution)/shard_map/jit(_take)/gather | solution.py:525
  3.2 1.0 multiply_reduce_fusion.1
  4.3 0.0 copy-start.1
  4.3 41.0 %shard_map.67 = (f32[1024,768]{1,0:T(8,128)}, f32[2,128,768]{2,1,0:T(8,128)}, f32[256,512]{1,0:T(8,128)}) custom-call(f32[256,768]{1,0:T(8,128)} %get-tuple-element.10.emb_ref, f32[256,256]{1,0:T(8,128)} %tgt_ref.1), custom_call_target="tpu_custom_call" | custom-call | tf_op jit(solution)/shard_map/pallas_call | solution.py:262
  45.3 0.0 copy-start.3
  45.3 2.3 %multiply_reduce_fusion = f32[1024]{0:T(1024)S(1)} fusion(f32[1024,768]{1,0:T(8,128)} %get-tuple-element.7.col_ref), kind=kLoop, calls=%fused_computation.1 | loop fusion | flops 1571840 | bytes 3149824 | tf_op jit(solution)/shard_map/reduce_sum | solution.py:23
  47.6 0.0 copy-done.1
  47.6 0.5 copy-done.3
  48.1 0.0 copy-start.4
  48.1 0.0 copy-start.2
  48.1 3.0 %fusion.4.slab_ref = f32[256,1024]{1,0:T(8,128)S(1)} fusion(f32[256,768]{1,0:T(8,128)S(1)} %copy-done.1, f32[1024,768]{1,0:T(8,128)S(1)} %copy-done.3, f32[]{:T(128)} %bitcast.7, s32[256]{0:T(256)S(1)} %fusion.6, f32[1024]{0:T(1024)S(1)} %multiply_reduce_fusion, f32[256]{0:T(256)S(1)} %get-tuple-element.9, pred[256]{0:T(512)(128)(4,1)S(1)} %compare_and_fusion), kind=kOutput, calls=%fused_computation.7 | convolution fusion | flops 2418278400 | bytes 4987140 | tf_op jit(solution)/shard_map/dot_general | solution.py:16
  51.1 0.0 copy-done.4
  51.2 1.9 %fusion.7 = f32[512,1024]{1,0:T(8,128)S(1)} fusion(f32[256,512]{1,0:T(8,128)S(1)} %copy-done.4, f32[256,1024]{1,0:T(8,128)S(1)} %fusion.4.slab_ref), kind=kOutput, calls=%fused_computation.18 | convolution fusion | flops 1610612736 | bytes 3670016 | tf_op jit(solution)/shard_map/dot_general | solution.py:534
  53.0 0.0 copy-done.2
  53.0 50.8 %shard_map.68 = (f32[32,1024]{1,0:T(8,128)S(1)}, f32[256,256]{1,0:T(8,128)S(1)}, f32[256,896]{1,0:T(8,128)S(1)}) custom-call(f32[1]{0:T(128)} %copy.10.ridge_ref, f32[16,32,1024]{2,1,0:T(8,128)S(1)} %bitcast.8, f32[256,768]{1,0:T(8,128)S(1)} %copy-done.1, f32[1024,768]{1,0:T(8,128)} %get-tuple-element.7.col_ref, f32[256,768]{1,0:T(8,128)S(1)} %bitcast.9, ...), custom_call_target="tpu_custom_call" | custom-call | tf_op jit(solution)/shard_map/pallas_call | solution.py:492
  103.8 0.7 copy.11
  104.5 0.7 copy.12
  105.2 0.9 copy.13
  (3 shorter events, 0.0 us)
Async XLA Ops:
  0.6 1.5 %copy-start = (f32[512,768]{1,0:T(8,128)S(1)}, f32[512,768]{1,0:T(8,128)}, u32[]{:S(2)}) copy-start(f32[512,768]{1,0:T(8,128)} %param.4) | copy-start | bytes 4718596
  4.3 43.4 %copy-start.1 = (f32[256,768]{1,0:T(8,128)S(1)}, f32[256,768]{1,0:T(8,128)}, u32[]{:S(2)}) copy-start(f32[256,768]{1,0:T(8,128)} %get-tuple-element.10.emb_ref) | copy-start | bytes 2359300
  45.3 2.8 %copy-start.3 = (f32[1024,768]{1,0:T(8,128)S(1)}, f32[1024,768]{1,0:T(8,128)}, u32[]{:S(2)}) copy-start(f32[1024,768]{1,0:T(8,128)} %get-tuple-element.7.col_ref) | copy-start | bytes 9437188
  48.1 3.0 %copy-start.4 = (f32[256,512]{1,0:T(8,128)S(1)}, f32[256,512]{1,0:T(8,128)}, u32[]{:S(2)}) copy-start(f32[256,512]{1,0:T(8,128)} %get-tuple-element.6) | copy-start | bytes 1572868
  48.1 4.9 %copy-start.2 = (f32[2,128,768]{2,1,0:T(8,128)S(1)}, f32[2,128,768]{2,1,0:T(8,128)}, u32[]{:S(2)}) copy-start(f32[2,128,768]{2,1,0:T(8,128)} %get-tuple-element.8) | copy-start | bytes 2359300

commit v7 on v6

--- a/solution.py
+++ b/solution.py
@@ -356,7 +356,7 @@
             c_plain_y(t).start()
 
     ends, middle = order[:2], order[2:]
-    ring_start(ends)
+    ring_start(order)
 
     heads = head_ref[...]
     heads_sq = dot_t(jnp.ones((8, heads.shape[1]), jnp.float32), heads * heads)[:1]
@@ -438,28 +438,26 @@
         return 0
 
 
-    for t in ends:
+    lax.fori_loop(0, half_cols // chunk, land_chunk, 0)
+    factor(0, 1)
+    for t in order:
         ring_sum(t)
-    ring_start(middle)
-    factor(0, 2)
-    for t in middle:
-        ring_sum(t)
+    factor(1, 3)
     for t in ends:
         ring_total(t)
     if lines > 1:
         line_step(0)
-    factor(2, 4)
+    factor(3, 4)
     for t in middle:
         ring_total(t)
     if lines > 2:
         line_step(1)
-    factor(4, 6)
+    factor(4, 5)
     if lines > 3:
         line_step(2)
-    factor(6, 8)
+    factor(5, 8)
     for step in range(3, lines - 1):
         line_step(step)
-    lax.fori_loop(0, half_cols // chunk, land_chunk, 0)
     lower = iota((n_head, n_head), 1) // BLOCK <= iota((n_head, n_head), 0) // BLOCK
     inverse = jnp.where(lower, work[...], 0.0)
     panels = dot_t(head_slab[...], inverse)

time: 106 us -> 104 us (0.981)
  Pallas kernels: 91.8 us -> 89.1 us
    pallas_call x1, Pallas kernels: 50.8 us -> 48.1 us  [finish(): pl.pallas_call(finish_kernel, out_shape=(jax.ShapeDtypeStruct((share, wid...]
where the time goes in v7:
time: 104 us; the launch traced here: 103 us
  Pallas kernels  89.1 us (86%)
  matrix products  4.85 us (5%)
  other arithmetic  4.05 us (4%)
  local copies, waits for them, and re-layouts  3.89 us (4%)
  between operations  1.51 us (1%)
    pallas_call x1, Pallas kernels, finish(): pl.pallas_call(finish_kernel, out_shape=(jax.ShapeDtypeStruct((share, wid...  48.1 us
    pallas_call x1, Pallas kernels, gather(): pl.pallas_call(gather_kernel, out_shape=(jax.ShapeDtypeStruct((C // 2, wi...  41 us
    dot_general x1, matrix products, dot_t(): lax.dot_general(left, right, (((1,), (1,)), ((), ())), precision=exact_mo...  3 us
    unnamed x13, local copies, waits for them, and re-layouts  2.8 us
    reduce_sum x1, other arithmetic, gaussian(): right_sq = jnp.sum(right_rows * right_rows, axis=1)  2.31 us

profile of v7, /device:TPU:8, one launch (start us, length us, event | category | flops | bytes accessed | tf_op | source)
XLA Modules:
  0.0 103.4 jit_solution(2484618707789325036)
XLA Ops:
  0.6 0.0 copy-start
  1.4 0.7 compare_and_fusion.1
  2.1 0.0 copy-done
  2.2 1.1 %gather_fusion = f32[256,768]{1,0:T(8,128)S(1)} fusion(f32[512,768]{1,0:T(8,128)S(1)} %copy-done, s32[1024]{0:T(1024)S(1)} %pad_clamp_fusion), kind=kCustom, calls=%fused_computation | custom fusion | bytes 1573888 | tf_op jit(solution)/shard_map/jit(_take)/gather | solution.py:523
  3.2 1.0 multiply_reduce_fusion.1
  4.3 0.0 copy-start.1
  4.3 41.0 %shard_map.67 = (f32[1024,768]{1,0:T(8,128)}, f32[2,128,768]{2,1,0:T(8,128)}, f32[256,512]{1,0:T(8,128)}) custom-call(f32[256,768]{1,0:T(8,128)} %get-tuple-element.10.emb_ref, f32[256,256]{1,0:T(8,128)} %tgt_ref.1), custom_call_target="tpu_custom_call" | custom-call | tf_op jit(solution)/shard_map/pallas_call | solution.py:262
  45.3 0.0 copy-start.3
  45.3 2.3 %multiply_reduce_fusion = f32[1024]{0:T(1024)S(1)} fusion(f32[1024,768]{1,0:T(8,128)} %get-tuple-element.7.col_ref), kind=kLoop, calls=%fused_computation.1 | loop fusion | flops 1571840 | bytes 3149824 | tf_op jit(solution)/shard_map/reduce_sum | solution.py:23
  47.6 0.0 copy-done.1
  47.6 0.5 copy-done.3
  48.1 0.0 copy-start.4
  48.1 0.0 copy-start.2
  48.1 3.0 %fusion.4.slab_ref = f32[256,1024]{1,0:T(8,128)S(1)} fusion(f32[256,768]{1,0:T(8,128)S(1)} %copy-done.1, f32[1024,768]{1,0:T(8,128)S(1)} %copy-done.3, f32[]{:T(128)} %bitcast.7, s32[256]{0:T(256)S(1)} %fusion.6, f32[1024]{0:T(1024)S(1)} %multiply_reduce_fusion, f32[256]{0:T(256)S(1)} %get-tuple-element.9, pred[256]{0:T(512)(128)(4,1)S(1)} %compare_and_fusion), kind=kOutput, calls=%fused_computation.7 | convolution fusion | flops 2418278400 | bytes 4987140 | tf_op jit(solution)/shard_map/dot_general | solution.py:16
  51.1 0.0 copy-done.4
  51.2 1.9 %fusion.7 = f32[512,1024]{1,0:T(8,128)S(1)} fusion(f32[256,512]{1,0:T(8,128)S(1)} %copy-done.4, f32[256,1024]{1,0:T(8,128)S(1)} %fusion.4.slab_ref), kind=kOutput, calls=%fused_computation.18 | convolution fusion | flops 1610612736 | bytes 3670016 | tf_op jit(solution)/shard_map/dot_general | solution.py:532
  53.0 0.0 copy-done.2
  53.0 48.1 %shard_map.68 = (f32[32,1024]{1,0:T(8,128)S(1)}, f32[256,256]{1,0:T(8,128)S(1)}, f32[256,896]{1,0:T(8,128)S(1)}) custom-call(f32[1]{0:T(128)} %copy.10.ridge_ref, f32[16,32,1024]{2,1,0:T(8,128)S(1)} %bitcast.8, f32[256,768]{1,0:T(8,128)S(1)} %copy-done.1, f32[1024,768]{1,0:T(8,128)} %get-tuple-element.7.col_ref, f32[256,768]{1,0:T(8,128)S(1)} %bitcast.9, ...), custom_call_target="tpu_custom_call" | custom-call | tf_op jit(solution)/shard_map/pallas_call | solution.py:490
  101.1 0.7 copy.11
  101.8 0.7 copy.12
  102.5 0.9 copy.13
  (3 shorter events, 0.0 us)
Async XLA Ops:
  0.6 1.5 %copy-start = (f32[512,768]{1,0:T(8,128)S(1)}, f32[512,768]{1,0:T(8,128)}, u32[]{:S(2)}) copy-start(f32[512,768]{1,0:T(8,128)} %param.4) | copy-start | bytes 4718596
  4.3 43.4 %copy-start.1 = (f32[256,768]{1,0:T(8,128)S(1)}, f32[256,768]{1,0:T(8,128)}, u32[]{:S(2)}) copy-start(f32[256,768]{1,0:T(8,128)} %get-tuple-element.10.emb_ref) | copy-start | bytes 2359300
  45.3 2.8 %copy-start.3 = (f32[1024,768]{1,0:T(8,128)S(1)}, f32[1024,768]{1,0:T(8,128)}, u32[]{:S(2)}) copy-start(f32[1024,768]{1,0:T(8,128)} %get-tuple-element.7.col_ref) | copy-start | bytes 9437188
  48.1 3.0 %copy-start.4 = (f32[256,512]{1,0:T(8,128)S(1)}, f32[256,512]{1,0:T(8,128)}, u32[]{:S(2)}) copy-start(f32[256,512]{1,0:T(8,128)} %get-tuple-element.6) | copy-start | bytes 1572868
  48.1 4.9 %copy-start.2 = (f32[2,128,768]{2,1,0:T(8,128)S(1)}, f32[2,128,768]{2,1,0:T(8,128)}, u32[]{:S(2)}) copy-start(f32[2,128,768]{2,1,0:T(8,128)} %get-tuple-element.8) | copy-start | bytes 2359300

commit v8 on v7

--- a/solution.py
+++ b/solution.py
@@ -50,20 +50,16 @@
     lane = iota((size, 128), 1)
     row = iota((size, 128), 0)
     pair = jnp.where(lane < size, rolled[:, :128], jnp.where(lane == row + size, 1.0, 0.0))
-    for j in range(0, size, 2):
-        k = j + 1
-        first_row, second_row = pair[j:k, :], pair[k : k + 1, :]
-        a, b, d = pair[j:k, j:k], pair[j:k, k : k + 1], pair[k : k + 1, k : k + 1]
-        scale = 1.0 / (a * d - b * b)
-        left = (d * first_row - b * second_row) * scale
-        right = (a * second_row - b * first_row) * scale
-        later = row > k
-        pair = (
-            pair
-            - jnp.where(later, pair[:, j:k], 0.0) * left
-            - jnp.where(later, pair[:, k : k + 1], 0.0) * right
-            - jnp.where(row == k, b / a, 0.0) * first_row
-        )
+    finished, rest = [], pair
+    for j in range(size - 1):
+        if j and j % 8 == 0:
+            finished.append(rest[:8, :])
+            rest = rest[8:, :]
+        at = j % 8
+        column = rest[:, j : j + 1]
+        scaled = rest[at : at + 1, :] / rest[at : at + 1, j : j + 1]
+        rest = rest - jnp.where(row[: rest.shape[0], :] > at, column, 0.0) * scaled
+    pair = jnp.concatenate(finished + [rest], axis=0)
     diagonal = jnp.sum(jnp.where(lane == row, pair, 0.0), axis=1, keepdims=True)
     block_inv = (pair / jnp.sqrt(diagonal))[:, size : 2 * size]
 

time: 104 us -> 102 us (0.981)
  Pallas kernels: 89.1 us -> 87.9 us
    pallas_call x1, Pallas kernels: 48.1 us -> 46.9 us  [finish(): pl.pallas_call(finish_kernel, out_shape=(jax.ShapeDtypeStruct((share, wid...]
where the time goes in v8:
time: 102 us
  Pallas kernels  87.9 us (86%)
  matrix products  4.85 us (5%)
  other arithmetic  4.05 us (4%)
  local copies, waits for them, and re-layouts  3.89 us (4%)
  between operations  1.51 us (1%)
    pallas_call x1, Pallas kernels, finish(): pl.pallas_call(finish_kernel, out_shape=(jax.ShapeDtypeStruct((share, wid...  46.9 us
    pallas_call x1, Pallas kernels, gather(): pl.pallas_call(gather_kernel, out_shape=(jax.ShapeDtypeStruct((C // 2, wi...  41 us
    dot_general x1, matrix products, dot_t(): lax.dot_general(left, right, (((1,), (1,)), ((), ())), precision=exact_mo...  3 us
    unnamed x13, local copies, waits for them, and re-layouts  2.8 us
    reduce_sum x1, other arithmetic, gaussian(): right_sq = jnp.sum(right_rows * right_rows, axis=1)  2.31 us

profile of v8, /device:TPU:8, one launch (start us, length us, event | category | flops | bytes accessed | tf_op | source)
XLA Modules:
  0.0 102.2 jit_solution(12942898864843876180)
XLA Ops:
  0.6 0.0 copy-start
  1.4 0.7 compare_and_fusion.1
  2.1 0.0 copy-done
  2.2 1.1 %gather_fusion = f32[256,768]{1,0:T(8,128)S(1)} fusion(f32[512,768]{1,0:T(8,128)S(1)} %copy-done, s32[1024]{0:T(1024)S(1)} %pad_clamp_fusion), kind=kCustom, calls=%fused_computation | custom fusion | bytes 1573888 | tf_op jit(solution)/shard_map/jit(_take)/gather | solution.py:519
  3.2 1.0 %multiply_reduce_fusion.1 = (f32[256]{0:T(256)S(1)}, f32[256,768]{1,0:T(8,128)}) fusion(f32[256,768]{1,0:T(8,128)S(1)} %gather_fusion, pred[256]{0:T(512)(128)(4,1)S(1)} %get-tuple-element.11), kind=kLoop, calls=%fused_computation.10 | loop fusion | flops 589568 | bytes 1574144 | tf_op jit(solution)/shard_map/reduce_sum | solution.py:22
  4.3 0.0 copy-start.1
  4.3 41.0 %shard_map.67 = (f32[1024,768]{1,0:T(8,128)}, f32[2,128,768]{2,1,0:T(8,128)}, f32[256,512]{1,0:T(8,128)}) custom-call(f32[256,768]{1,0:T(8,128)} %get-tuple-element.10.emb_ref, f32[256,256]{1,0:T(8,128)} %tgt_ref.1), custom_call_target="tpu_custom_call" | custom-call | tf_op jit(solution)/shard_map/pallas_call | solution.py:258
  45.3 0.0 copy-start.3
  45.3 2.3 %multiply_reduce_fusion = f32[1024]{0:T(1024)S(1)} fusion(f32[1024,768]{1,0:T(8,128)} %get-tuple-element.7.col_ref), kind=kLoop, calls=%fused_computation.1 | loop fusion | flops 1571840 | bytes 3149824 | tf_op jit(solution)/shard_map/reduce_sum | solution.py:23
  47.6 0.0 copy-done.1
  47.6 0.5 copy-done.3
  48.1 0.0 copy-start.4
  48.1 0.0 copy-start.2
  48.1 3.0 %fusion.4.slab_ref = f32[256,1024]{1,0:T(8,128)S(1)} fusion(f32[256,768]{1,0:T(8,128)S(1)} %copy-done.1, f32[1024,768]{1,0:T(8,128)S(1)} %copy-done.3, f32[]{:T(128)} %bitcast.7, s32[256]{0:T(256)S(1)} %fusion.6, f32[1024]{0:T(1024)S(1)} %multiply_reduce_fusion, f32[256]{0:T(256)S(1)} %get-tuple-element.9, pred[256]{0:T(512)(128)(4,1)S(1)} %compare_and_fusion), kind=kOutput, calls=%fused_computation.7 | convolution fusion | flops 2418278400 | bytes 4987140 | tf_op jit(solution)/shard_map/dot_general | solution.py:16
  51.1 0.0 copy-done.4
  51.2 1.9 %fusion.7 = f32[512,1024]{1,0:T(8,128)S(1)} fusion(f32[256,512]{1,0:T(8,128)S(1)} %copy-done.4, f32[256,1024]{1,0:T(8,128)S(1)} %fusion.4.slab_ref), kind=kOutput, calls=%fused_computation.18 | convolution fusion | flops 1610612736 | bytes 3670016 | tf_op jit(solution)/shard_map/dot_general | solution.py:528
  53.0 0.0 copy-done.2
  53.0 46.9 %shard_map.68 = (f32[32,1024]{1,0:T(8,128)S(1)}, f32[256,256]{1,0:T(8,128)S(1)}, f32[256,896]{1,0:T(8,128)S(1)}) custom-call(f32[1]{0:T(128)} %copy.10.ridge_ref, f32[16,32,1024]{2,1,0:T(8,128)S(1)} %bitcast.8, f32[256,768]{1,0:T(8,128)S(1)} %copy-done.1, f32[1024,768]{1,0:T(8,128)} %get-tuple-element.7.col_ref, f32[256,768]{1,0:T(8,128)S(1)} %bitcast.9, ...), custom_call_target="tpu_custom_call" | custom-call | tf_op jit(solution)/shard_map/pallas_call | solution.py:486
  99.9 0.7 copy.11
  100.6 0.7 copy.12
  101.3 0.9 copy.13
  (3 shorter events, 0.0 us)
Async XLA Ops:
  0.6 1.5 %copy-start = (f32[512,768]{1,0:T(8,128)S(1)}, f32[512,768]{1,0:T(8,128)}, u32[]{:S(2)}) copy-start(f32[512,768]{1,0:T(8,128)} %param.4) | copy-start | bytes 4718596
  4.3 43.4 %copy-start.1 = (f32[256,768]{1,0:T(8,128)S(1)}, f32[256,768]{1,0:T(8,128)}, u32[]{:S(2)}) copy-start(f32[256,768]{1,0:T(8,128)} %get-tuple-element.10.emb_ref) | copy-start | bytes 2359300
  45.3 2.8 %copy-start.3 = (f32[1024,768]{1,0:T(8,128)S(1)}, f32[1024,768]{1,0:T(8,128)}, u32[]{:S(2)}) copy-start(f32[1024,768]{1,0:T(8,128)} %get-tuple-element.7.col_ref) | copy-start | bytes 9437188
  48.1 3.0 %copy-start.4 = (f32[256,512]{1,0:T(8,128)S(1)}, f32[256,512]{1,0:T(8,128)}, u32[]{:S(2)}) copy-start(f32[256,512]{1,0:T(8,128)} %get-tuple-element.6) | copy-start | bytes 1572868
  48.1 4.9 %copy-start.2 = (f32[2,128,768]{2,1,0:T(8,128)S(1)}, f32[2,128,768]{2,1,0:T(8,128)}, u32[]{:S(2)}) copy-start(f32[2,128,768]{2,1,0:T(8,128)} %get-tuple-element.8) | copy-start | bytes 2359300

commit v9 on v8

--- a/solution.py
+++ b/solution.py
@@ -7,7 +7,7 @@
 
 C = 2048
 PW = 128
-BLOCK = 32
+BLOCK = 64
 
 exact_mode = lax.Precision.HIGHEST
 

time: 102 us -> 105 us (1.029)
  Pallas kernels: 87.9 us -> 90.5 us
    pallas_call x1, Pallas kernels: 46.9 us -> 49.5 us  [finish(): pl.pallas_call(finish_kernel, out_shape=(jax.ShapeDtypeStruct((share, wid...]
where the time goes in v9:
time: 105 us
  Pallas kernels  90.5 us (86%)
  matrix products  4.85 us (5%)
  other arithmetic  4.05 us (4%)
  local copies, waits for them, and re-layouts  3.89 us (4%)
  between operations  1.51 us (1%)
    pallas_call x1, Pallas kernels, finish(): pl.pallas_call(finish_kernel, out_shape=(jax.ShapeDtypeStruct((share, wid...  49.5 us
    pallas_call x1, Pallas kernels, gather(): pl.pallas_call(gather_kernel, out_shape=(jax.ShapeDtypeStruct((C // 2, wi...  41 us
    dot_general x1, matrix products, dot_t(): lax.dot_general(left, right, (((1,), (1,)), ((), ())), precision=exact_mo...  3 us
    unnamed x13, local copies, waits for them, and re-layouts  2.8 us
    reduce_sum x1, other arithmetic, gaussian(): right_sq = jnp.sum(right_rows * right_rows, axis=1)  2.31 us

profile of v9, /device:TPU:8, one launch (start us, length us, event | category | flops | bytes accessed | tf_op | source)
XLA Modules:
  0.0 104.9 jit_solution(79370919182979375)
XLA Ops:
  0.6 0.0 copy-start
  1.4 0.7 compare_and_fusion.1
  2.1 0.0 copy-done
  2.2 1.1 %gather_fusion = f32[256,768]{1,0:T(8,128)S(1)} fusion(f32[512,768]{1,0:T(8,128)S(1)} %copy-done, s32[1024]{0:T(1024)S(1)} %pad_clamp_fusion), kind=kCustom, calls=%fused_computation | custom fusion | bytes 1573888 | tf_op jit(solution)/shard_map/jit(_take)/gather | solution.py:519
  3.2 1.0 multiply_reduce_fusion.1
  4.3 0.0 copy-start.1
  4.3 41.0 %shard_map.67 = (f32[1024,768]{1,0:T(8,128)}, f32[2,128,768]{2,1,0:T(8,128)}, f32[256,512]{1,0:T(8,128)}) custom-call(f32[256,768]{1,0:T(8,128)} %get-tuple-element.10.emb_ref, f32[256,256]{1,0:T(8,128)} %tgt_ref.1), custom_call_target="tpu_custom_call" | custom-call | tf_op jit(solution)/shard_map/pallas_call | solution.py:258
  45.3 0.0 copy-start.3
  45.3 2.3 %multiply_reduce_fusion = f32[1024]{0:T(1024)S(1)} fusion(f32[1024,768]{1,0:T(8,128)} %get-tuple-element.7.col_ref), kind=kLoop, calls=%fused_computation.1 | loop fusion | flops 1571840 | bytes 3149824 | tf_op jit(solution)/shard_map/reduce_sum | solution.py:23
  47.6 0.0 copy-done.1
  47.6 0.5 copy-done.3
  48.1 0.0 copy-start.4
  48.1 0.0 copy-start.2
  48.1 3.0 %fusion.4.slab_ref = f32[256,1024]{1,0:T(8,128)S(1)} fusion(f32[256,768]{1,0:T(8,128)S(1)} %copy-done.1, f32[1024,768]{1,0:T(8,128)S(1)} %copy-done.3, f32[]{:T(128)} %bitcast.7, s32[256]{0:T(256)S(1)} %fusion.6, f32[1024]{0:T(1024)S(1)} %multiply_reduce_fusion, f32[256]{0:T(256)S(1)} %get-tuple-element.9, pred[256]{0:T(512)(128)(4,1)S(1)} %compare_and_fusion), kind=kOutput, calls=%fused_computation.7 | convolution fusion | flops 2418278400 | bytes 4987140 | tf_op jit(solution)/shard_map/dot_general | solution.py:16
  51.1 0.0 copy-done.4
  51.2 1.9 %fusion.7 = f32[512,1024]{1,0:T(8,128)S(1)} fusion(f32[256,512]{1,0:T(8,128)S(1)} %copy-done.4, f32[256,1024]{1,0:T(8,128)S(1)} %fusion.4.slab_ref), kind=kOutput, calls=%fused_computation.18 | convolution fusion | flops 1610612736 | bytes 3670016 | tf_op jit(solution)/shard_map/dot_general | solution.py:528
  53.0 0.0 copy-done.2
  53.0 49.5 %shard_map.68 = (f32[32,1024]{1,0:T(8,128)S(1)}, f32[256,256]{1,0:T(8,128)S(1)}, f32[256,896]{1,0:T(8,128)S(1)}) custom-call(f32[1]{0:T(128)} %copy.10.ridge_ref, f32[16,32,1024]{2,1,0:T(8,128)S(1)} %bitcast.8, f32[256,768]{1,0:T(8,128)S(1)} %copy-done.1, f32[1024,768]{1,0:T(8,128)} %get-tuple-element.7.col_ref, f32[256,768]{1,0:T(8,128)S(1)} %bitcast.9, ...), custom_call_target="tpu_custom_call" | custom-call | tf_op jit(solution)/shard_map/pallas_call | solution.py:486
  102.6 0.7 copy.11
  103.2 0.7 copy.12
  103.9 0.9 copy.13
  (3 shorter events, 0.0 us)
Async XLA Ops:
  0.6 1.5 %copy-start = (f32[512,768]{1,0:T(8,128)S(1)}, f32[512,768]{1,0:T(8,128)}, u32[]{:S(2)}) copy-start(f32[512,768]{1,0:T(8,128)} %param.4) | copy-start | bytes 4718596
  4.3 43.4 %copy-start.1 = (f32[256,768]{1,0:T(8,128)S(1)}, f32[256,768]{1,0:T(8,128)}, u32[]{:S(2)}) copy-start(f32[256,768]{1,0:T(8,128)} %get-tuple-element.10.emb_ref) | copy-start | bytes 2359300
  45.3 2.8 %copy-start.3 = (f32[1024,768]{1,0:T(8,128)S(1)}, f32[1024,768]{1,0:T(8,128)}, u32[]{:S(2)}) copy-start(f32[1024,768]{1,0:T(8,128)} %get-tuple-element.7.col_ref) | copy-start | bytes 9437188
  48.1 3.0 %copy-start.4 = (f32[256,512]{1,0:T(8,128)S(1)}, f32[256,512]{1,0:T(8,128)}, u32[]{:S(2)}) copy-start(f32[256,512]{1,0:T(8,128)} %get-tuple-element.6) | copy-start | bytes 1572868
  48.1 4.9 %copy-start.2 = (f32[2,128,768]{2,1,0:T(8,128)S(1)}, f32[2,128,768]{2,1,0:T(8,128)}, u32[]{:S(2)}) copy-start(f32[2,128,768]{2,1,0:T(8,128)} %get-tuple-element.8) | copy-start | bytes 2359300
